TPU v7x, 512 devices: a whole 4x4x16 slice. The times are simulated.
512 devices in a mesh: seq: 64 (over z, y_lo, core), tp: 8 (over y_hi, x).
Axes of the slice: x: 4, y: 4 (y_hi: 2, y_lo: 2; y = y_hi * 2 + y_lo), z: 16, core: 2. Of those that a mesh axis runs over, the one named last changes fastest.
Arguments:
- queries: bfloat16 [8192, 1024], P('seq'), may hold values from -8 to 8
- key_rows: bfloat16 [8192, 256], P(('seq', 'tp')), may hold values from -4 to 4
- value_rows: bfloat16 [8192, 256], P(('seq', 'tp')), may hold values from -6 to 6
- ssm_input: bfloat16 [8192, 3072], P('seq', 'tp'), may hold values from -0.29882812 to 0.29882812
- gate_input: bfloat16 [8192, 3072], P('seq', 'tp'), may hold values from -6 to 6
- write_vectors: bfloat16 [8192, 256], P('seq'), may hold values from -1.5 to 1.5
- read_vectors: bfloat16 [8192, 256], P('seq'), may hold values from -1.5 to 1.5
- decay_rates: float32 [8192, 48], P('seq', 'tp'), may hold values from 0 to 3, as said below
- attn_out_weight: bfloat16 [1024, 2048], P('tp'), may hold values from -0.8984375 to 0.8984375
- ssm_out_weight: bfloat16 [3072, 2048], P('tp'), may hold values from -0.109375 to 0.109375
Outputs:
- mixer_output: float32 [8192, 2048], P(('seq', 'tp'))
Inputs may be any that keep to these rules, and one draw needn't show every extreme that they name: `decay_rates`: positive.
All inputs are finite; a program needn't handle non-finite values.
Results may differ from a plain program's by a relative error of at most 0.0045.
Values may be sent and summed in bfloat16 or wider, within the bound.
No kernel may reach another device: no remote copies, remote signals or barrier semaphores. Data moves between devices by JAX's collectives and lax.ppermute only.
A program may use at most 128 MiB of HBM per device.

v0:
```python
import math

import jax
import jax.numpy as jnp
from jax import lax
from jax.sharding import PartitionSpec as P

ASKER_PROBES = 8
KVHEADS = 2
HEAD = 128


precise = lax.Precision.HIGHEST
masked_score = -1e30


def prefix(value, axis, join, neutral):
    count, mine = (lax.axis_size(axis), lax.axis_index(axis))
    pieces = jax.tree.map(lambda part: lax.all_gather(part, axis), value)
    so_far = jax.tree.map(
        lambda part, zero: jnp.full_like(part, 0) + jnp.asarray(zero, part.dtype), value, neutral
    )

    def turn(position, so_far):
        longer = join(so_far, jax.tree.map(lambda part: part[position], pieces))
        return jax.tree.map(lambda new, old: jnp.where(position < mine, new, old), longer, so_far)

    return lax.fori_loop(0, count - 1, turn, so_far)


def combined_all(value, axis, join):
    pieces = jax.tree.map(lambda part: lax.all_gather(part, axis), value)
    head = jax.tree.map(lambda part: part[0], pieces)
    tail = jax.tree.map(lambda part: part[1:], pieces)
    so_far, _ = lax.scan(lambda so_far, slab: (join(so_far, slab), None), head, tail)
    return so_far


def local_states(ssm_input, write_vectors, read_vectors, decay_rates):
    local_rows = ssm_input.shape[0]
    heads_here = decay_rates.shape[1]
    values_f32 = ssm_input.astype(jnp.float32).reshape(local_rows, heads_here, -1)
    write_f32 = write_vectors.astype(jnp.float32)
    read_f32 = read_vectors.astype(jnp.float32)
    decay_sum = jnp.cumsum(-decay_rates, axis=0)
    block_decay = decay_sum[-1]
    positions = jnp.arange(local_rows)
    causal = (positions[:, None] >= positions[None, :])[:, :, None]
    decay_gap = jnp.where(causal, decay_sum[:, None, :] - decay_sum[None, :, :], 0.0)
    read_write = jnp.dot(read_vectors, write_vectors.T, preferred_element_type=jnp.float32)
    factor = jnp.where(causal, jnp.exp(decay_gap), 0.0) * read_write[:, :, None]
    within = jnp.einsum("tsh,shp->thp", factor, values_f32, precision=precise)
    block_state = jnp.einsum(
        "sh,shp,sn->hpn",
        jnp.exp(block_decay[None, :] - decay_sum),
        values_f32,
        write_f32,
        precision=precise,
    )
    return (within, block_state, decay_sum, read_f32)


def combine_states(earlier, later):
    return (earlier[0] * later[0], later[0][:, None, None] * earlier[1] + later[1])


def join_partial(first_part, second_part):
    updated_peak = jnp.maximum(first_part[0], second_part[0])
    first_scale = jnp.exp(first_part[0] - updated_peak)
    second_scale = jnp.exp(second_part[0] - updated_peak)
    running_sum = first_part[1] * first_scale + second_part[1] * second_scale
    weighted = first_part[2] * first_scale[..., None] + second_part[2] * second_scale[..., None]
    return (updated_peak, running_sum, weighted)


def local(
    queries,
    key_rows,
    value_rows,
    ssm_input,
    gate_input,
    write_vectors,
    read_vectors,
    decay_rates,
    attn_out_weight,
    ssm_out_weight,
):
    local_rows = queries.shape[0]
    within, block_state, decay_sum, read_f32 = local_states(
        ssm_input, write_vectors, read_vectors, decay_rates
    )
    block_decay = jnp.exp(decay_sum[-1])
    neutral = (jnp.ones_like(block_decay), jnp.zeros_like(block_state))
    entering = prefix((block_decay, block_state), "seq", combine_states, neutral)
    carried = jnp.einsum(
        "th,tn,hpn->thp", jnp.exp(decay_sum), read_f32, entering[1], precision=precise
    )
    ssm_raw = (within + carried).reshape(local_rows, -1)
    ssm_half = (ssm_raw * jax.nn.silu(gate_input.astype(jnp.float32))).astype(jnp.bfloat16)
    group = ASKER_PROBES // KVHEADS
    query_heads = queries.reshape(local_rows, KVHEADS, group, HEAD)
    slice_rows = key_rows.shape[0]
    seq_index = lax.axis_index("seq")
    tp_index = lax.axis_index("tp")
    query_place = seq_index * local_rows + jnp.arange(local_rows)
    score_scale = 1.0 / math.sqrt(HEAD)
    start_max = jnp.full((local_rows, KVHEADS, group), masked_score, jnp.float32)
    start_sum = jnp.zeros((local_rows, KVHEADS, group), jnp.float32)
    start_weighted = jnp.zeros((local_rows, KVHEADS, group, HEAD), jnp.float32)
    running = (start_max, start_sum, start_weighted)
    first_row = jnp.int32(0)
    key_segment = lax.all_gather(key_rows, "seq", axis=0, tiled=True)
    value_part = lax.all_gather(value_rows, "seq", axis=0, tiled=True)
    piece_rows = key_segment.shape[0]
    for lower_row in range(0, piece_rows, 256):
        upper_row = min(lower_row + 256, piece_rows)
        attend_key_segment = key_segment[lower_row:upper_row]
        attend_value_part = value_part[lower_row:upper_row]
        attend_first_row = first_row + lower_row
        attend_piece_rows = attend_key_segment.shape[0]
        row_ids = attend_first_row + jnp.arange(attend_piece_rows)
        key_place = (
            row_ids // slice_rows * local_rows + tp_index * slice_rows + row_ids % slice_rows
        )
        compute_running_max, compute_running_sum, compute_weighted = running
        key_block = attend_key_segment.reshape(attend_piece_rows, KVHEADS, HEAD)
        value_block = attend_value_part.reshape(attend_piece_rows, KVHEADS, HEAD)
        scores = (
            jnp.einsum("tgqd,ngd->tgqn", query_heads, key_block, preferred_element_type=jnp.float32)
            * score_scale
        )
        visible = (key_place[None, :] <= query_place[:, None])[:, None, None, :]
        scores = jnp.where(visible, scores, masked_score)
        updated_peak = jnp.maximum(compute_running_max, jnp.max(scores, axis=-1))
        weights = jnp.where(visible, jnp.exp(scores - updated_peak[..., None]), 0.0)
        factor = jnp.exp(compute_running_max - updated_peak)
        compute_running_sum = compute_running_sum * factor + jnp.sum(weights, axis=-1)
        compute_weighted = compute_weighted * factor[..., None] + jnp.einsum(
            "tgqn,ngd->tgqd",
            weights.astype(jnp.bfloat16),
            value_block,
            preferred_element_type=jnp.float32,
        )
        running = (updated_peak, compute_running_sum, compute_weighted)
    running_max, running_sum, weighted = running
    heads_mine = ASKER_PROBES // lax.axis_size("tp")
    running_max, running_sum, weighted = combined_all(
        (running_max, running_sum, weighted), "tp", join_partial
    )
    all_heads = (weighted / running_sum[..., None]).reshape(local_rows, ASKER_PROBES, HEAD)
    own_heads = lax.dynamic_slice_in_dim(all_heads, tp_index * heads_mine, heads_mine, 1)
    attn_half = own_heads.reshape(local_rows, heads_mine * HEAD).astype(jnp.bfloat16)
    attention_share = lax.psum_scatter(
        jnp.dot(attn_half, attn_out_weight, preferred_element_type=jnp.float32),
        "tp",
        scatter_dimension=0,
        tiled=True,
    )
    state_share = lax.psum_scatter(
        jnp.dot(ssm_half, ssm_out_weight, preferred_element_type=jnp.float32),
        "tp",
        scatter_dimension=0,
        tiled=True,
    )
    summed = attention_share + state_share
    return summed


def solution(mesh):
    placed = (
        P("seq", None),
        P(("seq", "tp"), None),
        P(("seq", "tp"), None),
        P("seq", "tp"),
        P("seq", "tp"),
        P("seq", None),
        P("seq", None),
        P("seq", "tp"),
        P("tp", None),
        P("tp", None),
    )
    return jax.shard_map(
        local, mesh=mesh, in_specs=placed, out_specs=P(("seq", "tp"), None), check_vma=False
    )
```

profile of v0, /device:TPU:6, one launch (start us, length us, event | category | flops | bytes accessed | tf_op | source)
XLA Modules:
  0.0 597.0 jit_solution(9801647952218511953)
XLA Ops:
  6.6 1.2 reshape.438
  7.8 71.4 %all_gather.30 = bf16[1024,256]{1,0:T(8,128)(2,1)S(1)} all-gather(bf16[16,256]{1,0:T(8,128)(2,1)} %param.15), channel_id=1, replica_groups=mesh['seq'=64,'tp'=8] {'seq'}, dimensions={0}, use_global_device_ids=true | all-gather | bytes 532480 | tf_op jit(solution)/shard_map/all_gather | solution.py:112
  80.3 61.2 %all_gather.33 = bf16[1024,256]{1,0:T(8,128)(2,1)S(1)} all-gather(bf16[16,256]{1,0:T(8,128)(2,1)} %param.16), channel_id=1, replica_groups=mesh['seq'=64,'tp'=8] {'seq'}, dimensions={0}, use_global_device_ids=true | all-gather | bytes 532480 | tf_op jit(solution)/shard_map/all_gather | solution.py:113
  144.2 1.3 fusion.106
  148.0 1.7 fusion.19
  152.8 1.4 fusion.23
  154.2 1.4 fusion.25
  155.6 1.4 fusion.27
  158.0 34.1 %all_gather.32 = f32[8,128,2,4]{1,3,2,0:T(4,128)S(1)} all-gather(f32[1,128,2,4]{1,3,2,0:T(4,128)S(1)} %get-tuple-element.225), channel_id=1, replica_groups=mesh['seq'=64,'tp'=8] {'tp'}, dimensions={0}, use_global_device_ids=true | all-gather | bytes 36864 | tf_op jit(solution)/shard_map/all_gather | solution.py:32
  192.1 34.1 %all_gather.31 = f32[8,128,2,4]{1,3,2,0:T(4,128)S(1)} all-gather(f32[1,128,2,4]{1,3,2,0:T(4,128)S(1)} %get-tuple-element.226), channel_id=1, replica_groups=mesh['seq'=64,'tp'=8] {'tp'}, dimensions={0}, use_global_device_ids=true | all-gather | bytes 36864 | tf_op jit(solution)/shard_map/all_gather | solution.py:32
  226.2 63.2 %all-gather.2 = f32[64,1,6]{2,1,0:T(1,128)} all-gather(f32[1,1,6]{2,1,0:T(1,128)S(1)} %copy-done.21), channel_id=1, replica_groups=mesh['seq'=64,'tp'=8] {'seq'}, dimensions={0}, use_global_device_ids=true | all-gather | bytes 1560 | tf_op jit(solution)/shard_map/all_gather | solution.py:19
  289.5 1.3 convolution_bitcast_fusion.5
  292.3 4.2 slice.76
  296.4 18.6 %while.28 = (s32[]{:T(128)}, f32[128,2,4]{0,2,1:T(4,128)S(1)}, f32[128,2,4]{0,2,1:T(4,128)S(1)}, f32[128,2,4,128]{3,2,1,0:T(4,128)S(1)}, f32[7,128,2,4]{1,3,2,0:...) while((s32[]{:T(128)}, f32[128,2,4]{0,2,1:T(4,128)S(1)}, ...), condition=%wide.region_9.10_spmd, body=%wide.region_8.9_spmd.sunk | while | flops 399362 | bytes 2678885 | solution.py:35
  297.9 1.2 fusion.126
  300.5 1.2 fusion.126
  303.2 1.2 fusion.126
  305.9 1.2 fusion.126
  308.5 1.2 fusion.126
  311.2 1.2 fusion.126
  313.8 1.2 fusion.126
  315.9 72.0 %all-gather.8.cloned.1.call-done = f32[384,64,256]{2,1,0:T(8,128)} async-done(((f32[6,64,256]{2,1,0:T(8,128)}), f32[384,64,256]{2,1,0:T(8,128)}) %all-gather.8.cloned.1.call-update) | async-done | bytes 25165840 | tf_op jit(solution)/shard_map/all_gather | solution.py:19
  387.9 114.7 %while.29 = (s32[]{:T(128)}, f32[6,64,256]{2,1,0:T(8,128)S(1)}, s32[]{:T(128)}, f32[64,6]{1,0:T(8,128)}, f32[64,6,64,256]{3,2,1,0:T(8,128)}, /*index=5*/s32[]{:T(128)}, s32[]{:T(128)}) while((s32[]{:T(128)}, f32[6,64,256]{2,1,0:T(8,128)S(1)}, s32[]{:T(128)}, f32[64,6]{1,0:T(8,128)}, f32[64,6,64,256]{3,2,1,0:T(8,128)}, ...), condition=%wide.region_13.14_spmd.clone, body=%wide.region_12.13_spmd.clone.sunk | while | flops 393220 | bytes 1179833 | solution.py:28
  388.6 1.1 fusion.127
  390.4 1.1 fusion.127
  392.2 1.1 fusion.127
  423.2 1.1 fusion.127
  454.1 1.1 fusion.127
  461.4 1.1 fusion.127
  476.0 1.1 fusion.127
  503.1 2.3 convolution_add_fusion
  505.5 85.0 %reduce-scatter.2.cloned.1.call-done = f32[16,2048]{1,0:T(8,128)} async-done(((f32[128,2048]{1,0:T(8,128)}), f32[16,2048]{1,0:T(8,128)}) %reduce-scatter.2.cloned.1.call-update) | async-done | bytes 131088 | tf_op jit(solution)/shard_map/reduce_scatter | solution.py:153
  (248 shorter events, 128.1 us)
Async XLA Ops:
  6.5 496.6 %copy-start = (bf16[384,2048]{1,0:T(8,128)(2,1)S(1)}, bf16[384,2048]{1,0:T(8,128)(2,1)}, u32[]{:S(2)}) copy-start(bf16[384,2048]{1,0:T(8,128)(2,1)} %param.23) | copy-start | bytes 4718596
  6.5 284.3 %all-gather.6.cloned.1.call-start = ((), (), s32[]{:S(2)}) async-start(), calls=%async_computation.1 | async-start | bytes 4718592 | tf_op jit(solution)/shard_map/all_gather | solution.py:32
  143.9 2.7 copy-start.7
  144.2 2.9 copy-start.6
  145.5 2.1 copy-start.13
  145.5 2.1 copy-start.5
  145.9 1.2 copy-start.14
  145.9 2.1 copy-start.1
  146.2 1.7 copy-start.2
  146.3 1.7 copy-start.15
  146.6 1.3 copy-start.3
  146.6 1.3 copy-start.17
  147.1 2.6 copy-start.20
  147.1 3.5 copy-start.12
  147.1 3.7 copy-start.8
  149.7 139.7 %copy-start.9 = (bf16[128,256]{1,0:T(8,128)(2,1)S(1)}, bf16[128,256]{1,0:T(8,128)(2,1)}, u32[]{:S(2)}) copy-start(bf16[128,256]{1,0:T(8,128)(2,1)} %param.20) | copy-start | bytes 196612
  149.7 238.2 %all-gather.8.cloned.1.call-start = ((), (), s32[]{:S(2)}) async-start(), calls=%async_computation.2 | async-start | bytes 25559040 | tf_op jit(solution)/shard_map/all_gather | solution.py:19
  150.8 6.4 %copy-start.16 = (f32[128,2,4]{0,2,1:T(4,128)S(1)}, f32[128,2,4]{0,2,1:T(4,128)}, u32[]{:S(2)}) copy-start(f32[128,2,4]{0,2,1:T(4,128)} %copy-done.15) | copy-start | bytes 12292
  150.8 6.4 %copy-start.18 = (f32[128,2,4]{0,2,1:T(4,128)S(1)}, f32[128,2,4]{0,2,1:T(4,128)}, u32[]{:S(2)}) copy-start(f32[128,2,4]{0,2,1:T(4,128)} %copy-done.17) | copy-start | bytes 12292
  150.8 75.4 %copy-start.21 = (f32[1,1,6]{2,1,0:T(1,128)S(1)}, f32[1,1,6]{2,1,0:T(1,128)}, u32[]{:S(2)}) copy-start(f32[1,1,6]{2,1,0:T(1,128)} %get-tuple-element.224) | copy-start | bytes 76
  152.0 438.5 %reduce-scatter.2.cloned.1.call-start = ((), (), s32[]{:S(2)}) async-start(), calls=%async_computation.3 | async-start | bytes 1179648 | tf_op jit(solution)/shard_map/reduce_scatter | solution.py:153
  296.4 19.1 %copy-start.4 = (bf16[128,2048]{1,0:T(8,128)(2,1)S(1)}, bf16[128,2048]{1,0:T(8,128)(2,1)}, u32[]{:S(2)}) copy-start(bf16[128,2048]{1,0:T(8,128)(2,1)} %param.22) | copy-start | bytes 1572868
  315.6 187.0 %copy-start.19 = (f32[128,6]{0,1:T(8,128)S(1)}, f32[128,6]{0,1:T(8,128)}, u32[]{:S(2)}) copy-start(f32[128,6]{0,1:T(8,128)} %copy.97) | copy-start | bytes 9220
  315.9 186.7 %copy-start.10 = (bf16[128,256]{1,0:T(8,128)(2,1)S(1)}, bf16[128,256]{1,0:T(8,128)(2,1)}, u32[]{:S(2)}) copy-start(bf16[128,256]{1,0:T(8,128)(2,1)} %param.20) | copy-start | bytes 196612
  315.9 186.7 %copy-start.11 = (f32[128,6,64]{0,2,1:T(8,128)S(1)}, f32[128,6,64]{0,2,1:T(8,128)}, u32[]{:S(2)}) copy-start(f32[128,6,64]{0,2,1:T(8,128)} %convolution_bitcast_fusion.5) | copy-start | bytes 589828
Sparse Core Ops, SparseCore 0:
  149.8 80.8 all-gather.5
  232.9 154.9 all-gather.7
  505.6 84.8 reduce-scatter.1
where the time goes:
time: 602 us; the launch traced here: 597 us
  blocking collectives  264 us (44%)
  waiting for transfers between devices  157 us (26%)
  other arithmetic  84.3 us (14%)
  local copies, waits for them, and re-layouts  65.4 us (11%)
  between operations  13.6 us (2%)
  matrix products  10.7 us (2%)
    reduce_scatter x1, waiting for transfers between devices, local(): lax.psum_scatter(jnp.dot(attn_half, attn_out_weight, preferred_element_ty...  85 us
    all_gather x1, waiting for transfers between devices, prefix(): pieces = jax.tree.map(lambda part: lax.all_gather(part, axis), value)  72 us
    all_gather x1, blocking collectives, local(): key_segment = lax.all_gather(key_rows, 'seq', axis=0, tiled=True)  71.4 us
    select_n x63, other arithmetic, turn(): jnp.where(position < mine, new, old)  69.8 us
    all_gather x2, blocking collectives, combined_all(): pieces = jax.tree.map(lambda part: lax.all_gather(part, axis), value)  68.2 us
    all_gather x1, blocking collectives, prefix(): pieces = jax.tree.map(lambda part: lax.all_gather(part, axis), value)  63.2 us
    all_gather x1, blocking collectives, local(): value_part = lax.all_gather(value_rows, 'seq', axis=0, tiled=True)  61.2 us
    mul x63, local copies, waits for them, and re-layouts, combine_states(): later[0][:, None, None] * earlier[1] + later[1]  43.3 us
  transfers between devices with their start and end apart: 3, of which 2 were waited for; matrix products, arithmetic and copies ran while one was open for 6% of the time, Pallas kernels for 0%

commit v1 on v0

v1 whole, which is shorter than its diff:
```python
import math

import jax
import jax.numpy as jnp
from jax import lax
from jax.experimental import pallas as pl
from jax.experimental.pallas import tpu as pltpu
from jax.sharding import PartitionSpec as P

f32 = jnp.float32
bf16 = jnp.bfloat16
ROWS = 128
HEADS = 6
HDIM = 64
CH = HEADS * HDIM
STATE = 256
GROUP = 16
SUPER = 4
OWN = CH // GROUP
PAD = 32
HEAD = 128
QH = 8
TP = 8
SLICE = 16
D = 2048
LOW = -1e30
SCALE = 1.0 / math.sqrt(HEAD)
HI = lax.Precision.HIGHEST

near = [[GROUP * h + i for i in range(GROUP)] for h in range(SUPER)]
far = [[GROUP * h + i for h in range(SUPER)] for i in range(GROUP)]


def iota(shape, dim):
    return lax.broadcasted_iota(jnp.int32, shape, dim)


def cut(v, parts):
    out = []
    for _ in range(parts):
        hi = v.astype(bf16).astype(f32)
        out.append(hi)
        v = v - hi
    return out


def spread(r, shape, dim, width):
    which = iota(shape, dim) // width
    out = jnp.zeros(shape, f32)
    for h in range(HEADS):
        out = jnp.where(which == h, r[:, h : h + 1], out)
    return out


def nn(a, b):
    return lax.dot_general(a, b, (((1,), (0,)), ((), ())), preferred_element_type=f32)


def nt(a, b):
    return lax.dot_general(a, b, (((1,), (1,)), ((), ())), preferred_element_type=f32)


def tn(a, b):
    return lax.dot_general(a, b, (((0,), (0,)), ((), ())), preferred_element_type=f32)


def states_kernel(x_ref, b_ref, r_ref, out_ref):
    rates = r_ref[...]
    later = (iota((ROWS, ROWS), 1) > iota((ROWS, ROWS), 0)).astype(bf16)
    rx = spread(rates, (ROWS, CH), 1, HDIM)
    after = sum(nn(later, part.astype(bf16)) for part in cut(rx, 3))
    xs = x_ref[...].astype(f32) * jnp.exp(-after)
    hi, lo = cut(xs.T, 2)
    b = b_ref[...]
    state = nn(hi.astype(bf16), b) + nn(lo.astype(bf16), b)
    total = jnp.exp(-jnp.sum(rates, axis=0, keepdims=True))
    shape = (GROUP, 8, STATE)
    which = (iota(shape, 0) * OWN + iota(shape, 2)) // HDIM
    fac = jnp.zeros(shape, f32)
    for h in range(HEADS):
        fac = jnp.where(which == h, total[:, h : h + 1].reshape(1, 1, 1), fac)
    hi, lo = cut(fac, 2)
    sub = iota(shape, 1)
    fac = jnp.where(sub == 0, hi, jnp.where(sub == 1, lo, 0.0))
    fac = jnp.where(iota(shape, 2) < OWN, fac, 0.0)
    out_ref[...] = jnp.concatenate([state.reshape(GROUP, OWN, STATE), fac], axis=1).astype(bf16)


def unpack(block):
    block = block.astype(f32)
    state = block[:OWN]
    row = block[OWN : OWN + 1] + block[OWN + 1 : OWN + 2]
    shape = (OWN, HEAD)
    pick = iota(shape, 0) == iota(shape, 1)
    col = jnp.sum(jnp.where(pick, row[:, :HEAD], 0.0), axis=1, keepdims=True)
    return state, row, col


def decay_rows(row):
    hi, lo = cut(row, 2)
    sub = iota((8, STATE), 0)
    return jnp.where(sub == 0, hi, jnp.where(sub == 1, lo, 0.0))


def total_kernel(ra_ref, k_ref, v_ref, out_ref):
    state = jnp.zeros((OWN, STATE), f32)
    prod = jnp.ones((1, STATE), f32)
    for j in range(GROUP):
        s, row, col = unpack(ra_ref[j])
        state = col * state + s
        prod = prod * row
    packed = jnp.concatenate([state, decay_rows(prod)], axis=0).astype(bf16)
    for h in range(SUPER):
        out_ref[h, 0:SLICE, :] = k_ref[...]
        out_ref[h, SLICE : 2 * SLICE, :] = v_ref[...]
        out_ref[h, 2 * SLICE : 2 * SLICE + PAD, :] = packed


def enter_kernel(ra_ref, rb_ref, out_ref):
    mine = lax.axis_index("seq") // GROUP
    state = jnp.zeros((OWN, STATE), f32)
    for h in range(SUPER - 1):
        s, _, col = unpack(rb_ref[h, 2 * SLICE :, :])
        state = jnp.where(h < mine, col * state + s, state)
    kv = [
        jnp.concatenate([rb_ref[2 * c, 0 : 2 * SLICE, :], rb_ref[2 * c + 1, 0 : 2 * SLICE, :]], axis=0)
        for c in range(2)
    ]
    pad = jnp.zeros((PAD - OWN, STATE), f32)
    for j in range(GROUP):
        out_ref[j, 0:PAD, :] = jnp.concatenate([state, pad], axis=0).astype(bf16)
        out_ref[j, PAD:, :] = kv[j % 2]
        if j < GROUP - 1:
            s, _, col = unpack(ra_ref[j])
            state = col * state + s


def within_kernel(x_ref, g_ref, b_ref, c_ref, r_ref, a_out, b_out):
    rates = r_ref[...]
    keep = iota((ROWS, ROWS), 0) >= iota((ROWS, ROWS), 1)
    upto = keep.astype(bf16)
    gate = g_ref[...].astype(f32)
    sg = gate / (1.0 + jnp.exp(-gate))
    rp = spread(rates, (ROWS, ROWS), 1, 1)
    cs = sum(nn(upto, part.astype(bf16)) for part in cut(rp, 3))
    cst = cs.T
    b_out[...] = jnp.exp(-spread(cs, (ROWS, CH), 1, HDIM)) * sg
    cb = nt(c_ref[...], b_ref[...])
    left = iota((ROWS, 2 * HDIM), 1) < HDIM
    for p in range(HEADS // 2):
        xp = x_ref[:, 2 * HDIM * p : 2 * HDIM * (p + 1)]
        x2 = jnp.concatenate([jnp.where(left, xp, 0), jnp.where(left, 0, xp)], axis=0).astype(bf16)
        ms = []
        for h in (2 * p, 2 * p + 1):
            gap = jnp.where(keep, cst[h : h + 1, :] - cs[:, h : h + 1], LOW)
            ms.append(jnp.exp(gap) * cb)
        hi, lo = cut(jnp.concatenate(ms, axis=1), 2)
        y = nn(hi.astype(bf16), x2) + nn(lo.astype(bf16), x2)
        a_out[:, 2 * HDIM * p : 2 * HDIM * (p + 1)] = y * sg[:, 2 * HDIM * p : 2 * HDIM * (p + 1)]


def attention_kernel(q_ref, own_ref, other_ref, out_ref):
    seq, tp = lax.axis_index("seq"), lax.axis_index("tp")
    core = lax.rem(seq, 2)
    keys = GROUP * SLICE
    n = iota((keys, ROWS), 0)
    place = (n // SLICE) * ROWS + tp * SLICE + n % SLICE
    query = seq * ROWS + iota((keys, ROWS), 1)
    chunks = []
    for ref, half in ((own_ref, core), (other_ref, 1 - core)):
        for hh in range(2):
            first = (2 * half + hh) * (GROUP * ROWS)
            vis = place + first <= query
            chunks.append((ref, hh, jnp.concatenate([vis] * 4, axis=1)))
    for g in range(2):
        lanes = slice(g * HEAD, (g + 1) * HEAD)
        qg = jnp.concatenate(
            [q_ref[:, (4 * g + a) * HEAD : (4 * g + a + 1) * HEAD] for a in range(4)], axis=0
        )
        scores = []
        for ref, hh, vis in chunks:
            kk = ref[:, 32 * hh : 32 * hh + 16, lanes].reshape(keys, HEAD)
            scores.append(jnp.where(vis, nt(kk, qg), LOW))
        peak = scores[0]
        for s in scores[1:]:
            peak = jnp.maximum(peak, s)
        peak = jnp.maximum(jnp.max(peak, axis=0, keepdims=True), 0.1 * LOW)
        total = jnp.zeros((1, 4 * ROWS), f32)
        summed = jnp.zeros((HEAD, 4 * ROWS), f32)
        for s, (ref, hh, vis) in zip(scores, chunks):
            w = jnp.exp2((s - peak) * (SCALE * math.log2(math.e)))
            total = total + jnp.sum(w, axis=0, keepdims=True)
            vv = ref[:, 32 * hh + 16 : 32 * hh + 32, lanes].reshape(keys, HEAD)
            summed = summed + tn(vv, w.astype(bf16))
        parts = cut(peak * SCALE, 3) + cut(total, 3)
        sub = iota((16, 4 * ROWS), 0)
        stats = jnp.zeros((16, 4 * ROWS), f32)
        for k, part in enumerate(parts):
            stats = jnp.where(sub == k, part, stats)
        for a in range(4):
            cols = slice(a * ROWS, (a + 1) * ROWS)
            out_ref[4 * g + a, 0:HEAD, :] = summed[:, cols].astype(bf16)
            out_ref[4 * g + a, HEAD:, :] = stats[:, cols].astype(bf16)


def carry_kernel(s_ref, c_ref, a_ref, b_ref, w_ref, out_ref):
    state = s_ref[:, 0:PAD, :].astype(f32)[:, :OWN, :].reshape(CH, STATE).astype(bf16)
    y = a_ref[...] + b_ref[...] * nt(c_ref[...], state)
    y = y.astype(bf16)
    for k in range(D // 512):
        out_ref[:, 512 * k : 512 * (k + 1)] = nn(y, w_ref[:, 512 * k : 512 * (k + 1)])


def project_kernel(rd_ref, w_ref, p_ref, out_ref):
    peaks, totals = [], []
    for j in range(TP):
        stats = rd_ref[j, HEAD:, :].astype(f32)
        peaks.append(stats[0:1] + stats[1:2] + stats[2:3])
        totals.append(stats[3:4] + stats[4:5] + stats[5:6])
    peak = peaks[0]
    for p in peaks[1:]:
        peak = jnp.maximum(peak, p)
    total = jnp.zeros((1, ROWS), f32)
    summed = jnp.zeros((HEAD, ROWS), f32)
    for j in range(TP):
        scale = jnp.exp(peaks[j] - peak)
        total = total + totals[j] * scale
        summed = summed + rd_ref[j, 0:HEAD, :].astype(f32) * scale
    attn = (summed / total).T.astype(bf16)
    for k in range(D // 512):
        cols = slice(512 * k, 512 * (k + 1))
        out = nn(attn, w_ref[:, cols]) + p_ref[:, cols]
        out_ref[:, :, cols] = out.astype(bf16).reshape(TP, SLICE, 512)


def sum_kernel(re_ref, out_ref):
    out = re_ref[0].astype(f32)
    for j in range(1, TP):
        out = out + re_ref[j].astype(f32)
    out_ref[...] = out


def call(kernel, name, outs, args, flops=0, moved=0, exps=0):
    many = isinstance(outs, list)
    shapes = [jax.ShapeDtypeStruct(s, d) for s, d in (outs if many else [outs])]
    spec = pl.BlockSpec(memory_space=pltpu.VMEM)
    return pl.pallas_call(
        kernel,
        name=name,
        out_shape=shapes if many else shapes[0],
        in_specs=[spec] * len(args),
        out_specs=[spec] * len(shapes) if many else spec,
        compiler_params=pltpu.CompilerParams(vmem_limit_bytes=40 * 2**20),
        cost_estimate=pl.CostEstimate(flops=flops, bytes_accessed=moved, transcendentals=exps),
    )(*args)


def swap(x, axis, groups=None):
    return lax.all_to_all(x, axis, 0, 0, axis_index_groups=groups)


def local(queries, keys, values, x, gate, write, read, rates, w_attn, w_ssm):
    sent = call(states_kernel, "states", ((GROUP, PAD, STATE), bf16), (x, write, rates), 10**8, 10**6)
    ra = swap(sent, "seq", near)
    ya, yb = call(
        within_kernel,
        "within",
        [((ROWS, CH), f32), ((ROWS, CH), f32)],
        (x, gate, write, read, rates),
        10**9,
        10**7,
        2 * 10**5,
    )
    totals = call(total_kernel, "totals", ((SUPER, 64, STATE), bf16), (ra, keys, values), 10**7, 10**6)
    rb = swap(totals, "seq", far)
    enter = call(enter_kernel, "enter", ((GROUP, 96, STATE), bf16), (ra, rb), 10**7, 10**6)
    rc = swap(enter, "seq", near)
    own = rc[:, PAD:, :]
    other = lax.ppermute(own, "seq", [(i, i ^ 1) for i in range(GROUP * SUPER)])
    partial = call(
        attention_kernel,
        "attention",
        ((QH, HEAD + 16, ROWS), bf16),
        (queries, own, other),
        6 * 10**8,
        2 * 10**6,
        10**6,
    )
    rd = swap(partial, "tp")
    ssm = call(carry_kernel, "carry", ((ROWS, D), f32), (rc, read, ya, yb, w_ssm), 10**9, 10**7)
    share = call(project_kernel, "project", ((TP, SLICE, D), bf16), (rd, w_attn, ssm), 10**8, 2 * 10**6)
    re = swap(share, "tp")
    return call(sum_kernel, "total", ((SLICE, D), f32), (re,), 10**6, 10**6)


def solution(mesh):
    placed = (
        P("seq", None),
        P(("seq", "tp"), None),
        P(("seq", "tp"), None),
        P("seq", "tp"),
        P("seq", "tp"),
        P("seq", None),
        P("seq", None),
        P("seq", "tp"),
        P("tp", None),
        P("tp", None),
    )
    return jax.shard_map(
        local, mesh=mesh, in_specs=placed, out_specs=P(("seq", "tp"), None), check_vma=False
    )
```

time: 602 us -> 112 us (0.19)
  blocking collectives: 264 us -> 82.3 us
  waiting for transfers between devices: 157 us -> 6.94 us
  other arithmetic: 84.3 us -> 0 us
  local copies, waits for them, and re-layouts: 65.4 us -> 4.58 us
  between operations: 13.6 us -> 0.14 us
  matrix products: 10.7 us -> 0 us
  starting transfers between devices: 0.09 us -> 9.94 us
  Pallas kernels: 0 us -> 6.28 us
    all_gather x5 -> x0, blocking collectives: 264 us -> none  [the longest x1 71.4 us: local(): key_segment = lax.all_gather(key_rows, 'seq', axis=0, tiled=True)]
    reduce_scatter x1 -> x0, waiting for transfers between devices: 85 us -> none  [local(): lax.psum_scatter(jnp.dot(attn_half, attn_out_weight, preferred_element_ty...]
    all_to_all x0 -> x4, blocking collectives: none -> 82.3 us  [swap(): return lax.all_to_all(x, axis, 0, 0, axis_index_groups=groups)]
    all_gather x2 -> x0, waiting for transfers between devices: 72 us -> none  [the longest x1 72 us: prefix(): pieces = jax.tree.map(lambda part: lax.all_gather(part, axis), value)]
    select_n x63 -> x0, other arithmetic: 69.8 us -> none  [turn(): jnp.where(position < mine, new, old)]
    mul x63 -> x0, local copies, waits for them, and re-layouts: 43.3 us -> none  [combine_states(): later[0][:, None, None] * earlier[1] + later[1]]
    dot_general x14 -> x0, matrix products: 10.7 us -> none  [the longest x4 2.82 us: local(): jnp.einsum('tgqn,ngd->tgqd', weights.astype(jnp.bfloat16), value_block, p...]
    add x18 -> x0, other arithmetic: 9.21 us -> none  [the longest x7 8.3 us: join_partial(): first_part[2] * first_scale[..., None]]
  transfers between devices with their start and end apart: 3 -> 2, of which waited for: 2 -> 2; matrix products, arithmetic and copies ran while one was open for 6% -> 0% of each run, Pallas kernels for 0% -> 1%
where the time goes in v1:
time: 112 us; the launch traced here: 110 us
  blocking collectives  82.3 us (73%)
  starting transfers between devices  9.94 us (9%)
  waiting for transfers between devices  6.94 us (6%)
  Pallas kernels  6.28 us (6%)
  local copies, waits for them, and re-layouts  4.58 us (4%)
    all_to_all x4, blocking collectives, swap(): return lax.all_to_all(x, axis, 0, 0, axis_index_groups=groups)  82.3 us
    all_to_all x1, starting transfers between devices, swap(): return lax.all_to_all(x, axis, 0, 0, axis_index_groups=groups)  7.13 us
    pallas_call x8, Pallas kernels, call(): pl.pallas_call(kernel, name=name, out_shape=shapes if many else shapes[0]...  6.28 us
    all_to_all x1, waiting for transfers between devices, swap(): return lax.all_to_all(x, axis, 0, 0, axis_index_groups=groups)  5.43 us
    unnamed x23, local copies, waits for them, and re-layouts  4.54 us
    ppermute x1, starting transfers between devices, local(): other = lax.ppermute(own, 'seq', [(i, i ^ 1) for i in range(GROUP * SUPER)])  2.81 us
  transfers between devices with their start and end apart: 2, of which 2 were waited for; matrix products, arithmetic and copies ran while one was open for 0% of the time, Pallas kernels for 1%

profile of v1, /device:TPU:6, one launch (start us, length us, event | category | flops | bytes accessed | tf_op | source)
XLA Modules:
  0.0 110.2 jit_solution(8202460068275892370)
XLA Ops:
  0.0 0.8 copy.11.r_ref
  0.8 0.9 copy-done.2
  1.7 0.8 copy-done.5
  2.5 0.7 states.1
  3.3 16.9 %all_to_all.25.ra_ref = bf16[16,32,256]{2,1,0:T(8,128)(2,1)S(1)} all-to-all(bf16[16,32,256]{2,1,0:T(8,128)(2,1)S(1)} %states.1), channel_id=1, replica_groups={{0,8,16,24,32,40,48,56,64,72,80,88,96,104,112,120},{128,136,144,152,160..., dimensions={0} | all-to-all | bytes 524288 | tf_op jit(solution)/shard_map/all_to_all | solution.py:259
  20.1 0.7 copy-done.7
  20.8 0.7 copy-done.8
  21.5 0.1 totals.1
  21.7 27.3 %all_to_all.26.rb_ref = bf16[4,64,256]{2,1,0:T(8,128)(2,1)S(1)} all-to-all(bf16[4,64,256]{2,1,0:T(8,128)(2,1)S(1)} %totals.1), channel_id=1, replica_groups={{0,128,256,384},{8,136,264,392},{16,144,272,400},{24,152,280,408},{32,1..., dimensions={0} | all-to-all | bytes 262144 | tf_op jit(solution)/shard_map/all_to_all | solution.py:259
  48.9 0.1 enter.1
  49.1 0.0 copy-start.9
  49.1 24.0 %all_to_all.27.s_ref = bf16[16,96,256]{2,1,0:T(8,128)(2,1)S(1)} all-to-all(bf16[16,96,256]{2,1,0:T(8,128)(2,1)S(1)} %enter.1), channel_id=1, replica_groups={{0,8,16,24,32,40,48,56,64,72,80,88,96,104,112,120},{128,136,144,152,160..., dimensions={0} | all-to-all | bytes 1572864 | tf_op jit(solution)/shard_map/all_to_all | solution.py:259
  73.1 0.0 copy-start.3
  73.1 0.0 copy-start.4
  73.2 0.0 copy-start.6
  73.2 0.0 copy-start.10
  73.2 2.8 %collective-permute-start = (bf16[16,64,256]{2,1,0:T(8,128)(2,1)S(1)}, bf16[16,64,256]{2,1,0:T(8,128)(2,1)S(1)}, u32[]{:S(2)}, u32[]{:S(2)}) collective-permute-start(bf16[16,64,256]{2,1,0:T(8,128)(2,1)S(1)} %slice.4.own_ref), channel_id=1, source_target_pairs={{0,8},{8,0},{16,24},{24,16},{32,40},{40,32},{48,56},{56,48},{64,72... | collective-permute-start | bytes 1572872 | tf_op jit(solution)/shard_map/ppermute | solution.py:279
  76.0 1.5 %collective-permute-done.other_ref = bf16[16,64,256]{2,1,0:T(8,128)(2,1)S(1)} collective-permute-done((bf16[16,64,256]{2,1,0:T(8,128)(2,1)S(1)}, bf16[16,64,256]{2,1,0:T(8,128)(2,1)S(1)}, u32[]{:S(2)}, u32[]{:S(2)}) %collective-permute-start) | collective-permute-done | bytes 524320 | tf_op jit(solution)/shard_map/ppermute | solution.py:279
  77.5 0.0 copy-done.9
  77.5 2.7 %attention.1 = bf16[8,144,128]{2,1,0:T(8,128)(2,1)} custom-call(bf16[128,1024]{1,0:T(8,128)(2,1)S(1)} %copy-done.9, bf16[16,64,256]{2,1,0:T(8,128)(2,1)S(1)} %slice.4.own_ref, bf16[16,64,256]{2,1,0:T(8,128)(2,1)S(1)} %collective-permute-done.other_ref), custom_call_target="tpu_custom_call" | custom-call | flops 600000000 | bytes 2000000 | tf_op jit(solution)/shard_map/attention/pallas_call | solution.py:247
  80.3 7.1 %all-to-all-start.3 = ((bf16[8,144,128]{2,1,0:T(8,128)(2,1)}), bf16[8,144,128]{2,1,0:T(8,128)(2,1)S(1)}, u32[]{:S(2)}, u32[]{:S(2)}) async-start(bf16[8,144,128]{2,1,0:T(8,128)(2,1)} %attention.1), calls=%async_computation.3 | async-start | bytes 589824 | tf_op jit(solution)/shard_map/all_to_all | solution.py:259
  87.4 0.0 copy-done.3
  87.4 0.0 copy-done.4
  87.4 0.0 copy-done.6
  87.4 0.0 copy-start
  87.4 0.8 within.1
  88.2 0.6 copy-done
  88.8 0.6 carry.1.p_ref
  89.5 5.4 %all-to-all-done.3.rd_ref = bf16[8,144,128]{2,1,0:T(8,128)(2,1)S(1)} async-done(((bf16[8,144,128]{2,1,0:T(8,128)(2,1)}), bf16[8,144,128]{2,1,0:T(8,128)(2,1)S(1)}, u32[]{:S(2)}, u32[]{:S(2)}) %all-to-all-start.3) | async-done | bytes 294944 | tf_op jit(solution)/shard_map/all_to_all | solution.py:259
  94.9 0.4 project.1
  95.3 14.2 %all_to_all.28.re_ref = bf16[8,16,2048]{2,1,0:T(8,128)(2,1)S(1)} all-to-all(bf16[8,16,2048]{2,1,0:T(8,128)(2,1)S(1)} %project.1), channel_id=1, replica_groups=mesh['seq'=64,'tp'=8] {'tp'}, dimensions={0} | all-to-all | bytes 1048576 | tf_op jit(solution)/shard_map/all_to_all | solution.py:259
  109.5 0.7 total.1
  (8 shorter events, 0.0 us)
Async XLA Ops:
  0.8 0.9 copy-start.2
  1.7 0.8 copy-start.5
  20.1 0.7 copy-start.7
  20.8 0.7 copy-start.8
  49.1 28.4 %copy-start.9 = (bf16[128,1024]{1,0:T(8,128)(2,1)S(1)}, bf16[128,1024]{1,0:T(8,128)(2,1)}, u32[]{:S(2)}) copy-start(bf16[128,1024]{1,0:T(8,128)(2,1)} %q_ref.1) | copy-start | bytes 786436
  73.1 14.3 %copy-start.3 = (bf16[128,384]{1,0:T(8,128)(2,1)S(1)}, bf16[128,384]{1,0:T(8,128)(2,1)}, u32[]{:S(2)}) copy-start(bf16[128,384]{1,0:T(8,128)(2,1)} %x_ref.3) | copy-start | bytes 294916
  73.1 14.3 %copy-start.4 = (bf16[128,256]{1,0:T(8,128)(2,1)S(1)}, bf16[128,256]{1,0:T(8,128)(2,1)}, u32[]{:S(2)}) copy-start(bf16[128,256]{1,0:T(8,128)(2,1)} %c_ref.3) | copy-start | bytes 196612
  73.2 14.2 %copy-start.6 = (bf16[128,256]{1,0:T(8,128)(2,1)S(1)}, bf16[128,256]{1,0:T(8,128)(2,1)}, u32[]{:S(2)}) copy-start(bf16[128,256]{1,0:T(8,128)(2,1)} %b_ref.3) | copy-start | bytes 196612
  73.2 14.2 %copy-start.10 = (bf16[128,384]{1,0:T(8,128)(2,1)S(1)}, bf16[128,384]{1,0:T(8,128)(2,1)}, u32[]{:S(2)}) copy-start(bf16[128,384]{1,0:T(8,128)(2,1)} %g_ref.1) | copy-start | bytes 294916
  73.2 4.3 %collective-permute-start = (bf16[16,64,256]{2,1,0:T(8,128)(2,1)S(1)}, bf16[16,64,256]{2,1,0:T(8,128)(2,1)S(1)}, u32[]{:S(2)}, u32[]{:S(2)}) collective-permute-start(bf16[16,64,256]{2,1,0:T(8,128)(2,1)S(1)} %slice.4.own_ref), channel_id=1, source_target_pairs={{0,8},{8,0},{16,24},{24,16},{32,40},{40,32},{48,56},{56,48},{64,72... | collective-permute-start | bytes 1572872 | tf_op jit(solution)/shard_map/ppermute | solution.py:279
  80.3 14.6 %all-to-all-start.3 = ((bf16[8,144,128]{2,1,0:T(8,128)(2,1)}), bf16[8,144,128]{2,1,0:T(8,128)(2,1)S(1)}, u32[]{:S(2)}, u32[]{:S(2)}) async-start(bf16[8,144,128]{2,1,0:T(8,128)(2,1)} %attention.1), calls=%async_computation.3 | async-start | bytes 589824 | tf_op jit(solution)/shard_map/all_to_all | solution.py:259
  87.4 1.4 %copy-start = (bf16[384,2048]{1,0:T(8,128)(2,1)S(1)}, bf16[384,2048]{1,0:T(8,128)(2,1)}, u32[]{:S(2)}) copy-start(bf16[384,2048]{1,0:T(8,128)(2,1)} %w_ref.2) | copy-start | bytes 4718596
  88.8 6.1 %copy-start.1 = (bf16[128,2048]{1,0:T(8,128)(2,1)S(1)}, bf16[128,2048]{1,0:T(8,128)(2,1)}, u32[]{:S(2)}) copy-start(bf16[128,2048]{1,0:T(8,128)(2,1)} %w_ref.3) | copy-start | bytes 1572868

commit v2 on v1

v2 whole, which is shorter than its diff:
```python
import math

import jax
import jax.numpy as jnp
from jax import lax
from jax.experimental import pallas as pl
from jax.experimental.pallas import tpu as pltpu
from jax.sharding import PartitionSpec as P

f32 = jnp.float32
bf16 = jnp.bfloat16
ROWS = 128
HEADS = 6
HDIM = 64
CH = HEADS * HDIM
STATE = 256
GROUP = 16
SUPER = 4
OWN = CH // GROUP
PAD = 32
HEAD = 128
TP = 8
SLICE = 16
D = 2048
LOW = -1e30
SCALE = 1.0 / math.sqrt(HEAD)
LOG2 = SCALE * math.log2(math.e)
KV = 64

near = [[GROUP * h + i for i in range(GROUP)] for h in range(SUPER)]
far = [[GROUP * h + i for h in range(SUPER)] for i in range(GROUP)]
row = [[0, 1, 2, 3], [4, 5, 6, 7]]


def iota(shape, dim):
    return lax.broadcasted_iota(jnp.int32, shape, dim)


def cut(v, parts):
    out = []
    for _ in range(parts):
        hi = v.astype(bf16).astype(f32)
        out.append(hi)
        v = v - hi
    return out


def spread(r, shape, dim, width):
    which = iota(shape, dim) // width
    out = jnp.zeros(shape, f32)
    for h in range(HEADS):
        out = jnp.where(which == h, r[:, h : h + 1], out)
    return out


def by_token(r):
    return jnp.concatenate([r, jnp.zeros((ROWS - HEADS, ROWS), f32)], axis=0).T


def nn(a, b):
    return lax.dot_general(a, b, (((1,), (0,)), ((), ())), preferred_element_type=f32)


def nt(a, b):
    return lax.dot_general(a, b, (((1,), (1,)), ((), ())), preferred_element_type=f32)


def tn(a, b):
    return lax.dot_general(a, b, (((0,), (0,)), ((), ())), preferred_element_type=f32)


def states_kernel(
    x_hbm, b_hbm, r_hbm, k_hbm, v_hbm, out_ref, keep_ref, give_ref, x_ref, b_ref, r_ref, k_ref, v_ref, sems
):
    copies = [
        pltpu.make_async_copy(source, target, sems.at[k])
        for k, (source, target) in enumerate(
            [(r_hbm, r_ref), (x_hbm, x_ref), (b_hbm, b_ref), (k_hbm, k_ref), (v_hbm, v_ref)]
        )
    ]
    for copy in copies:
        copy.start()
    for copy in copies:
        copy.wait()
    first = lax.axis_index("tp") < TP // 2
    kv = [
        jnp.concatenate([k_ref[:, HEAD * g : HEAD * (g + 1)], v_ref[:, HEAD * g : HEAD * (g + 1)]], axis=1)
        for g in range(2)
    ]
    keep_ref[...] = jnp.where(first, kv[0], kv[1])
    give_ref[...] = jnp.where(first, kv[1], kv[0])
    rates = by_token(r_ref[...])
    later = (iota((ROWS, ROWS), 1) > iota((ROWS, ROWS), 0)).astype(bf16)
    rx = spread(rates, (ROWS, CH), 1, HDIM)
    after = sum(nn(later, part.astype(bf16)) for part in cut(rx, 3))
    xs = x_ref[...].astype(f32) * jnp.exp(-after)
    hi, lo = cut(xs.T, 2)
    b = b_ref[...]
    state = nn(hi.astype(bf16), b) + nn(lo.astype(bf16), b)
    total = jnp.exp(-jnp.sum(rates, axis=0, keepdims=True))
    shape = (GROUP, 8, STATE)
    which = (iota(shape, 0) * OWN + iota(shape, 2)) // HDIM
    fac = jnp.zeros(shape, f32)
    for h in range(HEADS):
        fac = jnp.where(which == h, total[:, h : h + 1].reshape(1, 1, 1), fac)
    hi, lo = cut(fac, 2)
    sub = iota(shape, 1)
    fac = jnp.where(sub == 0, hi, jnp.where(sub == 1, lo, 0.0))
    fac = jnp.where(iota(shape, 2) < OWN, fac, 0.0)
    out_ref[...] = jnp.concatenate([state.reshape(GROUP, OWN, STATE), fac], axis=1).astype(bf16)


def unpack(block):
    block = block.astype(f32)
    state = block[:OWN]
    row = block[OWN : OWN + 1] + block[OWN + 1 : OWN + 2]
    shape = (OWN, HEAD)
    pick = iota(shape, 0) == iota(shape, 1)
    col = jnp.sum(jnp.where(pick, row[:, :HEAD], 0.0), axis=1, keepdims=True)
    return state, row, col


def decay_rows(row):
    hi, lo = cut(row, 2)
    sub = iota((8, STATE), 0)
    return jnp.where(sub == 0, hi, jnp.where(sub == 1, lo, 0.0))


def total_kernel(ra_ref, keep_ref, got_ref, out_ref):
    state = jnp.zeros((OWN, STATE), f32)
    prod = jnp.ones((1, STATE), f32)
    for j in range(GROUP):
        s, row, col = unpack(ra_ref[j])
        state = col * state + s
        prod = prod * row
    packed = jnp.concatenate([state, decay_rows(prod)], axis=0).astype(bf16)
    for h in range(SUPER):
        out_ref[h, 0:SLICE, :] = keep_ref[...]
        out_ref[h, SLICE : 2 * SLICE, :] = got_ref[...]
        out_ref[h, 2 * SLICE : 2 * SLICE + PAD, :] = packed


def enter_kernel(ra_ref, rb_ref, out_ref):
    mine = lax.axis_index("seq") // GROUP
    state = jnp.zeros((OWN, STATE), f32)
    for h in range(SUPER - 1):
        s, _, col = unpack(rb_ref[h, 2 * SLICE :, :])
        state = jnp.where(h < mine, col * state + s, state)
    kv = [
        jnp.concatenate([rb_ref[2 * c, 0 : 2 * SLICE, :], rb_ref[2 * c + 1, 0 : 2 * SLICE, :]], axis=0).astype(f32)
        for c in range(2)
    ]
    for j in range(GROUP):
        out_ref[j] = jnp.concatenate([kv[j % 2], state], axis=0).astype(bf16)
        if j < GROUP - 1:
            s, _, col = unpack(ra_ref[j])
            state = col * state + s


def within_kernel(x_ref, g_ref, b_ref, c_ref, r_ref, a_out, b_out):
    keep = iota((ROWS, ROWS), 0) >= iota((ROWS, ROWS), 1)
    upto = keep.astype(bf16)
    gate = g_ref[...].astype(f32)
    sg = gate / (1.0 + jnp.exp(-gate))
    cs = sum(nn(upto, part.astype(bf16)) for part in cut(by_token(r_ref[...]), 3))
    cst = cs.T
    b_out[...] = jnp.exp(-spread(cs, (ROWS, CH), 1, HDIM)) * sg
    cb = nt(c_ref[...], b_ref[...])
    left = iota((ROWS, 2 * HDIM), 1) < HDIM
    for p in range(HEADS // 2):
        xp = x_ref[:, 2 * HDIM * p : 2 * HDIM * (p + 1)]
        x2 = jnp.concatenate([jnp.where(left, xp, 0), jnp.where(left, 0, xp)], axis=0).astype(bf16)
        ms = []
        for h in (2 * p, 2 * p + 1):
            gap = jnp.where(keep, cst[h : h + 1, :] - cs[:, h : h + 1], LOW)
            ms.append(jnp.exp(gap) * cb)
        hi, lo = cut(jnp.concatenate(ms, axis=1), 2)
        y = nn(hi.astype(bf16), x2) + nn(lo.astype(bf16), x2)
        a_out[:, 2 * HDIM * p : 2 * HDIM * (p + 1)] = y * sg[:, 2 * HDIM * p : 2 * HDIM * (p + 1)]


def attend(q_ref, kv_ref, half, before):
    seq, tp = lax.axis_index("seq"), lax.axis_index("tp")
    keys = GROUP * 2 * SLICE
    n = iota((keys, ROWS), 0)
    in_pair = n % (2 * SLICE)
    slot = jnp.where(in_pair < SLICE, tp, lax.rem(tp + TP // 2, TP))
    place = (n // (2 * SLICE)) * ROWS + slot * SLICE + n % SLICE
    query = seq * ROWS + iota((keys, ROWS), 1)
    first = tp < TP // 2
    qg = jnp.concatenate(
        [
            jnp.where(first, q_ref[:, a * HEAD : (a + 1) * HEAD], q_ref[:, (4 + a) * HEAD : (5 + a) * HEAD])
            for a in range(4)
        ],
        axis=0,
    )
    scores = []
    for hh in range(2):
        vis = place + (2 * half + hh) * (GROUP * ROWS) <= query
        kk = kv_ref[:, 32 * hh : 32 * hh + 32, 0:HEAD].reshape(keys, HEAD)
        scores.append(jnp.where(jnp.concatenate([vis] * 4, axis=1), nt(kk, qg), LOW))
    peak = jnp.max(jnp.maximum(scores[0], scores[1]), axis=0, keepdims=True)
    peak = jnp.maximum(peak, 0.1 * LOW)
    if before is None:
        total = jnp.zeros((1, 4 * ROWS), f32)
        summed = jnp.zeros((HEAD, 4 * ROWS), f32)
    else:
        old, total, summed = before
        peak = jnp.maximum(peak, old)
        shrink = jnp.exp2((old - peak) * LOG2)
        total, summed = total * shrink, summed * shrink
    for hh in range(2):
        w = jnp.exp2((scores[hh] - peak) * LOG2)
        total = total + jnp.sum(w, axis=0, keepdims=True)
        vv = kv_ref[:, 32 * hh : 32 * hh + 32, HEAD:].reshape(keys, HEAD)
        summed = summed + tn(vv, w.astype(bf16))
    return peak, total, summed


def first_kernel(q_ref, kv_ref, sum_out, stat_out):
    peak, total, summed = attend(q_ref, kv_ref, lax.rem(lax.axis_index("seq"), 2), None)
    sum_out[...] = summed
    stat_out[...] = jnp.where(iota((8, 4 * ROWS), 0) == 0, peak, total)


def second_kernel(q_ref, kv_ref, sum_ref, stat_ref, out_ref):
    before = (stat_ref[0:1, :], stat_ref[1:2, :], sum_ref[...])
    peak, total, summed = attend(q_ref, kv_ref, 1 - lax.rem(lax.axis_index("seq"), 2), before)
    sub = iota((16, 4 * ROWS), 0)
    stats = jnp.zeros((16, 4 * ROWS), f32)
    for k, part in enumerate(cut(peak * SCALE, 3) + cut(total, 3)):
        stats = jnp.where(sub == k, part, stats)
    for a in range(4):
        cols = slice(a * ROWS, (a + 1) * ROWS)
        out_ref[a, 0:HEAD, :] = summed[:, cols].astype(bf16)
        out_ref[a, HEAD:, :] = stats[:, cols].astype(bf16)


def carry_kernel(s_ref, c_ref, a_ref, b_ref, w_ref, after_ref, out_ref):
    state = s_ref[...].astype(f32)[:, KV:, :].reshape(CH, STATE).astype(bf16)
    y = a_ref[...] + b_ref[...] * nt(c_ref[...], state)
    y = y.astype(bf16)
    for k in range(D // 512):
        out_ref[:, 512 * k : 512 * (k + 1)] = nn(y, w_ref[:, 512 * k : 512 * (k + 1)])


def project_kernel(rd_ref, w_ref, p_ref, out_ref):
    peaks, totals = [], []
    for j in range(TP // 2):
        stats = rd_ref[j, HEAD:, :].astype(f32)
        peaks.append(stats[0:1] + stats[1:2] + stats[2:3])
        totals.append(stats[3:4] + stats[4:5] + stats[5:6])
    peak = peaks[0]
    for p in peaks[1:]:
        peak = jnp.maximum(peak, p)
    total = jnp.zeros((1, ROWS), f32)
    summed = jnp.zeros((HEAD, ROWS), f32)
    for j in range(TP // 2):
        scale = jnp.exp(peaks[j] - peak)
        total = total + totals[j] * scale
        summed = summed + rd_ref[j, 0:HEAD, :].astype(f32) * scale
    attn = (summed / total).T.astype(bf16)
    for k in range(D // 512):
        cols = slice(512 * k, 512 * (k + 1))
        out = nn(attn, w_ref[:, cols]) + p_ref[:, cols]
        out_ref[:, :, cols] = out.astype(bf16).reshape(TP, SLICE, 512)


def sum_kernel(re_ref, out_ref):
    out = re_ref[0].astype(f32)
    for j in range(1, TP):
        out = out + re_ref[j].astype(f32)
    out_ref[...] = out


def call(kernel, name, outs, args, flops=0, moved=0, exps=0, left=(), scratch=(), vmem=40):
    many = isinstance(outs, list)
    shapes = [jax.ShapeDtypeStruct(s, d) for s, d in (outs if many else [outs])]
    spec = pl.BlockSpec(memory_space=pltpu.VMEM)
    return pl.pallas_call(
        kernel,
        name=name,
        out_shape=shapes if many else shapes[0],
        in_specs=[pl.BlockSpec(memory_space=pl.ANY) if k in left else spec for k in range(len(args))],
        out_specs=[spec] * len(shapes) if many else spec,
        scratch_shapes=list(scratch),
        compiler_params=pltpu.CompilerParams(vmem_limit_bytes=vmem * 2**20),
        cost_estimate=pl.CostEstimate(flops=flops, bytes_accessed=moved, transcendentals=exps),
    )(*args)


def swap(x, axis, groups=None):
    return lax.all_to_all(x, axis, 0, 0, axis_index_groups=groups)


def local(queries, keys, values, x, gate, write, read, rates, w_attn, w_ssm):
    rates = rates.T
    sent, keep, give = call(
        states_kernel,
        "states",
        [((GROUP, PAD, STATE), bf16), ((SLICE, 2 * HEAD), bf16), ((SLICE, 2 * HEAD), bf16)],
        (x, write, rates, keys, values),
        10**8,
        10**6,
        left=range(5),
        vmem=60,
        scratch=[
            pltpu.VMEM((ROWS, CH), bf16),
            pltpu.VMEM((ROWS, STATE), bf16),
            pltpu.VMEM((HEADS, ROWS), f32),
            pltpu.VMEM((SLICE, 2 * HEAD), bf16),
            pltpu.VMEM((SLICE, 2 * HEAD), bf16),
            pltpu.SemaphoreType.DMA((5,)),
        ],
    )
    ra = swap(sent, "seq", near)
    got = lax.ppermute(give, "tp", [(i, i ^ 4) for i in range(TP)])
    ya, yb = call(
        within_kernel,
        "within",
        [((ROWS, CH), f32), ((ROWS, CH), f32)],
        (x, gate, write, read, rates),
        10**9,
        10**7,
        2 * 10**5,
    )
    totals = call(total_kernel, "totals", ((SUPER, 64, STATE), bf16), (ra, keep, got), 10**7, 10**6)
    rb = swap(totals, "seq", far)
    enter = call(enter_kernel, "enter", ((GROUP, KV + OWN, STATE), bf16), (ra, rb), 10**7, 10**6)
    rc = swap(enter, "seq", near)
    own = rc[:, :KV, :]
    other = lax.ppermute(own, "seq", [(i, i ^ 1) for i in range(GROUP * SUPER)])
    summed, stats = call(
        first_kernel,
        "attend_own",
        [((HEAD, 4 * ROWS), f32), ((8, 4 * ROWS), f32)],
        (queries, own),
        3 * 10**8,
        2 * 10**6,
        5 * 10**5,
    )
    partial = call(
        second_kernel,
        "attend_other",
        ((TP // 2, HEAD + 16, ROWS), bf16),
        (queries, other, summed, stats),
        3 * 10**8,
        2 * 10**6,
        5 * 10**5,
    )
    rd = swap(partial, "tp", row)
    ssm = call(
        carry_kernel, "carry", ((ROWS, D), f32), (rc, read, ya, yb, w_ssm, partial), 10**9, 10**7, left=(5,)
    )
    share = call(project_kernel, "project", ((TP, SLICE, D), bf16), (rd, w_attn, ssm), 10**8, 2 * 10**6)
    re = swap(share, "tp")
    return call(sum_kernel, "total", ((SLICE, D), f32), (re,), 10**6, 10**6)


def solution(mesh):
    placed = (
        P("seq", None),
        P(("seq", "tp"), None),
        P(("seq", "tp"), None),
        P("seq", "tp"),
        P("seq", "tp"),
        P("seq", None),
        P("seq", None),
        P("seq", "tp"),
        P("tp", None),
        P("tp", None),
    )
    return jax.shard_map(
        local, mesh=mesh, in_specs=placed, out_specs=P(("seq", "tp"), None), check_vma=False
    )
```

time: 112 us -> 103 us (0.920)
  blocking collectives: 82.3 us -> 65 us
  starting transfers between devices: 9.94 us -> 19.4 us
  local copies, waits for them, and re-layouts: 4.58 us -> 1.48 us
  Pallas kernels: 6.28 us -> 8.02 us
    all_to_all x4 -> x3, blocking collectives: 82.3 us -> 65 us  [swap(): return lax.all_to_all(x, axis, 0, 0, axis_index_groups=groups)]
    ppermute x0 -> x1, starting transfers between devices: none -> 4.81 us  [local(): got = lax.ppermute(give, 'tp', [(i, i ^ 4) for i in range(TP)])]
    all_to_all x1 -> x2, starting transfers between devices: 7.13 us -> 11.8 us  [swap(): return lax.all_to_all(x, axis, 0, 0, axis_index_groups=groups)]
    unnamed x23 -> x18, local copies, waits for them, and re-layouts: 4.54 us -> 1.43 us
    ppermute x0 -> x1, waiting for transfers between devices: none -> 2.55 us  [local(): got = lax.ppermute(give, 'tp', [(i, i ^ 4) for i in range(TP)])]
    pallas_call x8 -> x9, Pallas kernels: 6.28 us -> 8.02 us  [call(): pl.pallas_call(kernel, name=name, out_shape=shapes if many else shapes[0]...]
    all_to_all x1 -> x2, waiting for transfers between devices: 5.43 us -> 4.62 us  [swap(): return lax.all_to_all(x, axis, 0, 0, axis_index_groups=groups)]
  transfers between devices with their start and end apart: 2 -> 4, of which waited for: 2 -> 4; matrix products, arithmetic and copies ran while one was open for 0% -> 0% of each run, Pallas kernels for 1% -> 2%
where the time goes in v2:
time: 103 us; the launch traced here: 102 us
  blocking collectives  65 us (63%)
  starting transfers between devices  19.4 us (19%)
  Pallas kernels  8.02 us (8%)
  waiting for transfers between devices  7.64 us (7%)
  local copies, waits for them, and re-layouts  1.48 us (1%)
    all_to_all x3, blocking collectives, swap(): return lax.all_to_all(x, axis, 0, 0, axis_index_groups=groups)  65 us
    all_to_all x2, starting transfers between devices, swap(): return lax.all_to_all(x, axis, 0, 0, axis_index_groups=groups)  11.8 us
    pallas_call x9, Pallas kernels, call(): pl.pallas_call(kernel, name=name, out_shape=shapes if many else shapes[0]...  8.02 us
    ppermute x1, starting transfers between devices, local(): got = lax.ppermute(give, 'tp', [(i, i ^ 4) for i in range(TP)])  4.81 us
    all_to_all x2, waiting for transfers between devices, swap(): return lax.all_to_all(x, axis, 0, 0, axis_index_groups=groups)  4.62 us
    ppermute x1, starting transfers between devices, local(): other = lax.ppermute(own, 'seq', [(i, i ^ 1) for i in range(GROUP * SUPER)])  2.73 us
    ppermute x1, waiting for transfers between devices, local(): got = lax.ppermute(give, 'tp', [(i, i ^ 4) for i in range(TP)])  2.55 us
  transfers between devices with their start and end apart: 4, of which 4 were waited for; matrix products, arithmetic and copies ran while one was open for 0% of the time, Pallas kernels for 2%

profile of v2, /device:TPU:6, one launch (start us, length us, event | category | flops | bytes accessed | tf_op | source)
XLA Modules:
  0.0 101.7 jit_solution(5655639728454804116)
XLA Ops:
  0.0 2.5 %states.1 = (bf16[16,32,256]{2,1,0:T(8,128)(2,1)}, bf16[16,256]{1,0:T(8,128)(2,1)}, bf16[16,256]{1,0:T(8,128)(2,1)}) custom-call(bf16[128,384]{1,0:T(8,128)(2,1)} %x_ref.1, bf16[128,256]{1,0:T(8,128)(2,1)} %b_ref.1, f32[6,128]{1,0:T(8,128)} %bitcast.1, bf16[16,256]{1,0:T(8,128)(2,1)} %k_hbm.1, bf16[16,256]{1,0:T(8,128)(2,1)} %v_hbm.1), custom_call_target="tpu_custom_call" | custom-call | flops 100000000 | bytes 1000000 | tf_op jit(solution)/shard_map/states/pallas_call | solution.py:281
  2.5 7.0 %all-to-all-start = ((bf16[16,32,256]{2,1,0:T(8,128)(2,1)}), bf16[16,32,256]{2,1,0:T(8,128)(2,1)S(1)}, u32[]{:S(2)}, u32[]{:S(2)}) async-start(bf16[16,32,256]{2,1,0:T(8,128)(2,1)} %get-tuple-element.12), calls=%async_computation | async-start | bytes 524288 | tf_op jit(solution)/shard_map/all_to_all | solution.py:294
  9.5 4.8 %collective-permute-start = (bf16[16,256]{1,0:T(8,128)(2,1)}, bf16[16,256]{1,0:T(8,128)(2,1)S(1)}, u32[]{:S(2)}, u32[]{:S(2)}) collective-permute-start(bf16[16,256]{1,0:T(8,128)(2,1)} %get-tuple-element.14), channel_id=1, source_target_pairs={{0,4},{1,5},{2,6},{3,7},{4,0},{5,1},{6,2},{7,3},{8,12},{9,13},{10,... | collective-permute-start | bytes 24584 | tf_op jit(solution)/shard_map/ppermute | solution.py:318
  14.4 2.5 %collective-permute-done.got_ref = bf16[16,256]{1,0:T(8,128)(2,1)S(1)} collective-permute-done((bf16[16,256]{1,0:T(8,128)(2,1)}, bf16[16,256]{1,0:T(8,128)(2,1)S(1)}, u32[]{:S(2)}, u32[]{:S(2)}) %collective-permute-start) | collective-permute-done | bytes 8224 | tf_op jit(solution)/shard_map/ppermute | solution.py:318
  16.9 2.7 %all-to-all-done.ra_ref = bf16[16,32,256]{2,1,0:T(8,128)(2,1)S(1)} async-done(((bf16[16,32,256]{2,1,0:T(8,128)(2,1)}), bf16[16,32,256]{2,1,0:T(8,128)(2,1)S(1)}, u32[]{:S(2)}, u32[]{:S(2)}) %all-to-all-start) | async-done | bytes 262176 | tf_op jit(solution)/shard_map/all_to_all | solution.py:294
  19.6 0.7 copy-done.4
  20.3 0.1 totals.1
  20.4 27.3 %all_to_all.25.rb_ref = bf16[4,64,256]{2,1,0:T(8,128)(2,1)S(1)} all-to-all(bf16[4,64,256]{2,1,0:T(8,128)(2,1)S(1)} %totals.1), channel_id=1, replica_groups={{0,128,256,384},{8,136,264,392},{16,144,272,400},{24,152,280,408},{32,1..., dimensions={0} | all-to-all | bytes 262144 | tf_op jit(solution)/shard_map/all_to_all | solution.py:294
  47.7 0.1 enter.1
  47.8 22.1 %all_to_all.26.s_ref = bf16[16,88,256]{2,1,0:T(8,128)(2,1)S(1)} all-to-all(bf16[16,88,256]{2,1,0:T(8,128)(2,1)S(1)} %enter.1), channel_id=1, replica_groups={{0,8,16,24,32,40,48,56,64,72,80,88,96,104,112,120},{128,136,144,152,160..., dimensions={0} | all-to-all | bytes 1441792 | tf_op jit(solution)/shard_map/all_to_all | solution.py:294
  70.0 0.0 copy-start.3
  70.0 0.0 copy-start.5
  70.0 0.0 copy-start.6
  70.0 0.0 copy-start.7
  70.0 0.0 copy-start.8
  70.0 2.7 %collective-permute-start.1 = (bf16[16,64,256]{2,1,0:T(8,128)(2,1)S(1)}, bf16[16,64,256]{2,1,0:T(8,128)(2,1)S(1)}, u32[]{:S(2)}, u32[]{:S(2)}) collective-permute-start(bf16[16,64,256]{2,1,0:T(8,128)(2,1)S(1)} %slice.4.kv_ref), channel_id=1, source_target_pairs={{0,8},{8,0},{16,24},{24,16},{32,40},{40,32},{48,56},{56,48},{64,72... | collective-permute-start | bytes 1572872 | tf_op jit(solution)/shard_map/ppermute | solution.py:333
  72.8 0.0 copy-done.2
  72.8 1.0 %attend_own.1 = (f32[128,512]{1,0:T(8,128)S(1)}, f32[8,512]{1,0:T(8,128)S(1)}) custom-call(bf16[128,1024]{1,0:T(8,128)(2,1)S(1)} %copy-done.2, bf16[16,64,256]{2,1,0:T(8,128)(2,1)S(1)} %slice.4.kv_ref), custom_call_target="tpu_custom_call" | custom-call | flops 300000000 | bytes 2000000 | tf_op jit(solution)/shard_map/attend_own/pallas_call | solution.py:281
  73.8 0.5 collective-permute-done.1.kv_ref
  74.3 1.8 %attend_other.1.after_ref = bf16[4,144,128]{2,1,0:T(8,128)(2,1)} custom-call(bf16[128,1024]{1,0:T(8,128)(2,1)S(1)} %copy-done.2, bf16[16,64,256]{2,1,0:T(8,128)(2,1)S(1)} %collective-permute-done.1.kv_ref, f32[128,512]{1,0:T(8,128)S(1)} %get-tuple-element.15.sum_ref, f32[8,512]{1,0:T(8,128)S(1)} %get-tuple-element.16.stat_ref), custom_call_target="tpu_custom_call" | custom-call | flops 300000000 | bytes 2000000 | tf_op jit(solution)/shard_map/attend_other/pallas_call | solution.py:281
  76.1 4.8 %all-to-all-start.3 = ((bf16[4,144,128]{2,1,0:T(8,128)(2,1)}), bf16[4,144,128]{2,1,0:T(8,128)(2,1)S(1)}, u32[]{:S(2)}, u32[]{:S(2)}) async-start(bf16[4,144,128]{2,1,0:T(8,128)(2,1)} %attend_other.1.after_ref), calls=%async_computation.3 | async-start | bytes 294912 | tf_op jit(solution)/shard_map/all_to_all | solution.py:294
  80.9 0.0 copy-done.3
  80.9 0.0 copy-done.5
  80.9 0.0 copy-done.6
  81.0 0.0 copy-start
  81.0 0.7 within.1
  81.7 0.7 copy-done
  82.4 0.6 carry.1.p_ref
  83.0 1.9 %all-to-all-done.3.rd_ref = bf16[4,144,128]{2,1,0:T(8,128)(2,1)S(1)} async-done(((bf16[4,144,128]{2,1,0:T(8,128)(2,1)}), bf16[4,144,128]{2,1,0:T(8,128)(2,1)S(1)}, u32[]{:S(2)}, u32[]{:S(2)}) %all-to-all-start.3) | async-done | bytes 147488 | tf_op jit(solution)/shard_map/all_to_all | solution.py:294
  84.9 0.4 project.1
  85.3 15.7 %all_to_all.27.re_ref = bf16[8,16,2048]{2,1,0:T(8,128)(2,1)S(1)} all-to-all(bf16[8,16,2048]{2,1,0:T(8,128)(2,1)S(1)} %project.1), channel_id=1, replica_groups=mesh['seq'=64,'tp'=8] {'tp'}, dimensions={0} | all-to-all | bytes 1048576 | tf_op jit(solution)/shard_map/all_to_all | solution.py:294
  101.0 0.7 total.1
  (7 shorter events, 0.1 us)
Async XLA Ops:
  2.5 17.1 %all-to-all-start = ((bf16[16,32,256]{2,1,0:T(8,128)(2,1)}), bf16[16,32,256]{2,1,0:T(8,128)(2,1)S(1)}, u32[]{:S(2)}, u32[]{:S(2)}) async-start(bf16[16,32,256]{2,1,0:T(8,128)(2,1)} %get-tuple-element.12), calls=%async_computation | async-start | bytes 524288 | tf_op jit(solution)/shard_map/all_to_all | solution.py:294
  9.5 7.4 %collective-permute-start = (bf16[16,256]{1,0:T(8,128)(2,1)}, bf16[16,256]{1,0:T(8,128)(2,1)S(1)}, u32[]{:S(2)}, u32[]{:S(2)}) collective-permute-start(bf16[16,256]{1,0:T(8,128)(2,1)} %get-tuple-element.14), channel_id=1, source_target_pairs={{0,4},{1,5},{2,6},{3,7},{4,0},{5,1},{6,2},{7,3},{8,12},{9,13},{10,... | collective-permute-start | bytes 24584 | tf_op jit(solution)/shard_map/ppermute | solution.py:318
  19.6 0.7 copy-start.4
  47.7 25.1 %copy-start.2 = (bf16[128,1024]{1,0:T(8,128)(2,1)S(1)}, bf16[128,1024]{1,0:T(8,128)(2,1)}, u32[]{:S(2)}) copy-start(bf16[128,1024]{1,0:T(8,128)(2,1)} %q_ref.3) | copy-start | bytes 786436
  70.0 10.9 %copy-start.3 = (bf16[128,256]{1,0:T(8,128)(2,1)S(1)}, bf16[128,256]{1,0:T(8,128)(2,1)}, u32[]{:S(2)}) copy-start(bf16[128,256]{1,0:T(8,128)(2,1)} %c_ref.3) | copy-start | bytes 196612
  70.0 10.9 %copy-start.5 = (bf16[128,384]{1,0:T(8,128)(2,1)S(1)}, bf16[128,384]{1,0:T(8,128)(2,1)}, u32[]{:S(2)}) copy-start(bf16[128,384]{1,0:T(8,128)(2,1)} %x_ref.1) | copy-start | bytes 294916
  70.0 10.9 %copy-start.6 = (bf16[128,384]{1,0:T(8,128)(2,1)S(1)}, bf16[128,384]{1,0:T(8,128)(2,1)}, u32[]{:S(2)}) copy-start(bf16[128,384]{1,0:T(8,128)(2,1)} %g_ref.1) | copy-start | bytes 294916
  70.0 10.9 %copy-start.7 = (bf16[128,256]{1,0:T(8,128)(2,1)S(1)}, bf16[128,256]{1,0:T(8,128)(2,1)}, u32[]{:S(2)}) copy-start(bf16[128,256]{1,0:T(8,128)(2,1)} %b_ref.1) | copy-start | bytes 196612
  70.0 10.9 %copy-start.8 = (f32[128,6]{0,1:T(8,128)S(1)}, f32[128,6]{0,1:T(8,128)}, u32[]{:S(2)}) copy-start(f32[128,6]{0,1:T(8,128)} %param.17) | copy-start | bytes 9220
  70.0 4.3 %collective-permute-start.1 = (bf16[16,64,256]{2,1,0:T(8,128)(2,1)S(1)}, bf16[16,64,256]{2,1,0:T(8,128)(2,1)S(1)}, u32[]{:S(2)}, u32[]{:S(2)}) collective-permute-start(bf16[16,64,256]{2,1,0:T(8,128)(2,1)S(1)} %slice.4.kv_ref), channel_id=1, source_target_pairs={{0,8},{8,0},{16,24},{24,16},{32,40},{40,32},{48,56},{56,48},{64,72... | collective-permute-start | bytes 1572872 | tf_op jit(solution)/shard_map/ppermute | solution.py:333
  76.1 8.8 %all-to-all-start.3 = ((bf16[4,144,128]{2,1,0:T(8,128)(2,1)}), bf16[4,144,128]{2,1,0:T(8,128)(2,1)S(1)}, u32[]{:S(2)}, u32[]{:S(2)}) async-start(bf16[4,144,128]{2,1,0:T(8,128)(2,1)} %attend_other.1.after_ref), calls=%async_computation.3 | async-start | bytes 294912 | tf_op jit(solution)/shard_map/all_to_all | solution.py:294
  81.0 1.4 %copy-start = (bf16[384,2048]{1,0:T(8,128)(2,1)S(1)}, bf16[384,2048]{1,0:T(8,128)(2,1)}, u32[]{:S(2)}) copy-start(bf16[384,2048]{1,0:T(8,128)(2,1)} %w_ref.2) | copy-start | bytes 4718596
  82.4 2.6 %copy-start.1 = (bf16[128,2048]{1,0:T(8,128)(2,1)S(1)}, bf16[128,2048]{1,0:T(8,128)(2,1)}, u32[]{:S(2)}) copy-start(bf16[128,2048]{1,0:T(8,128)(2,1)} %w_ref.3) | copy-start | bytes 1572868

commit v3 on v2

--- a/solution.py
+++ b/solution.py
@@ -19,17 +19,23 @@
 OWN = CH // GROUP
 PAD = 32
 HEAD = 128
+QUERY = 1024
 TP = 8
 SLICE = 16
 D = 2048
 LOW = -1e30
 SCALE = 1.0 / math.sqrt(HEAD)
 LOG2 = SCALE * math.log2(math.e)
-KV = 64
+KV = 32
 
 near = [[GROUP * h + i for i in range(GROUP)] for h in range(SUPER)]
 far = [[GROUP * h + i for h in range(SUPER)] for i in range(GROUP)]
-row = [[0, 1, 2, 3], [4, 5, 6, 7]]
+heads = [
+    [(4 * z + 2 * y_lo + core) * TP + 4 * y_hi + x for y_lo in range(2) for x in range(4)]
+    for z in range(GROUP * SUPER // 4)
+    for core in range(2)
+    for y_hi in range(2)
+]
 
 
 def iota(shape, dim):
@@ -140,18 +146,20 @@
         out_ref[h, 2 * SLICE : 2 * SLICE + PAD, :] = packed
 
 
-def enter_kernel(ra_ref, rb_ref, out_ref):
+def pick_kernel(q_ref, after_ref, out_ref):
+    half = QUERY // 2
+    out_ref[...] = jnp.where(lax.axis_index("tp") < TP // 2, q_ref[:, :half], q_ref[:, half:])
+
+
+def enter_kernel(ra_ref, rb_ref, after_ref, out_ref):
     mine = lax.axis_index("seq") // GROUP
     state = jnp.zeros((OWN, STATE), f32)
     for h in range(SUPER - 1):
         s, _, col = unpack(rb_ref[h, 2 * SLICE :, :])
         state = jnp.where(h < mine, col * state + s, state)
-    kv = [
-        jnp.concatenate([rb_ref[2 * c, 0 : 2 * SLICE, :], rb_ref[2 * c + 1, 0 : 2 * SLICE, :]], axis=0).astype(f32)
-        for c in range(2)
-    ]
+    kv = [rb_ref[h, 0:KV, :].astype(f32) for h in range(SUPER)]
     for j in range(GROUP):
-        out_ref[j] = jnp.concatenate([kv[j % 2], state], axis=0).astype(bf16)
+        out_ref[j] = jnp.concatenate([kv[j % SUPER], state], axis=0).astype(bf16)
         if j < GROUP - 1:
             s, _, col = unpack(ra_ref[j])
             state = col * state + s
@@ -179,59 +187,49 @@
         a_out[:, 2 * HDIM * p : 2 * HDIM * (p + 1)] = y * sg[:, 2 * HDIM * p : 2 * HDIM * (p + 1)]
 
 
-def attend(q_ref, kv_ref, half, before):
+def attend(q_ref, p_ref, kv_ref, part, before):
     seq, tp = lax.axis_index("seq"), lax.axis_index("tp")
-    keys = GROUP * 2 * SLICE
+    lower = lax.rem(seq // 2, 2) == 0
+    low_seq = jnp.where(lower, seq, seq - 2)
+    keys = GROUP * KV
     n = iota((keys, ROWS), 0)
-    in_pair = n % (2 * SLICE)
-    slot = jnp.where(in_pair < SLICE, tp, lax.rem(tp + TP // 2, TP))
-    place = (n // (2 * SLICE)) * ROWS + slot * SLICE + n % SLICE
-    query = seq * ROWS + iota((keys, ROWS), 1)
-    first = tp < TP // 2
-    qg = jnp.concatenate(
-        [
-            jnp.where(first, q_ref[:, a * HEAD : (a + 1) * HEAD], q_ref[:, (4 + a) * HEAD : (5 + a) * HEAD])
-            for a in range(4)
-        ],
-        axis=0,
-    )
-    scores = []
-    for hh in range(2):
-        vis = place + (2 * half + hh) * (GROUP * ROWS) <= query
-        kk = kv_ref[:, 32 * hh : 32 * hh + 32, 0:HEAD].reshape(keys, HEAD)
-        scores.append(jnp.where(jnp.concatenate([vis] * 4, axis=1), nt(kk, qg), LOW))
-    peak = jnp.max(jnp.maximum(scores[0], scores[1]), axis=0, keepdims=True)
-    peak = jnp.maximum(peak, 0.1 * LOW)
-    if before is None:
-        total = jnp.zeros((1, 4 * ROWS), f32)
-        summed = jnp.zeros((HEAD, 4 * ROWS), f32)
-    else:
-        old, total, summed = before
-        peak = jnp.maximum(peak, old)
-        shrink = jnp.exp2((old - peak) * LOG2)
-        total, summed = total * shrink, summed * shrink
-    for hh in range(2):
-        w = jnp.exp2((scores[hh] - peak) * LOG2)
-        total = total + jnp.sum(w, axis=0, keepdims=True)
-        vv = kv_ref[:, 32 * hh : 32 * hh + 32, HEAD:].reshape(keys, HEAD)
-        summed = summed + tn(vv, w.astype(bf16))
+    slot = jnp.where(n % KV < SLICE, tp, lax.rem(tp + TP // 2, TP))
+    place = (n // KV) * ROWS + slot * SLICE + n % SLICE + part * (GROUP * ROWS)
+    query = low_seq * ROWS + iota((keys, ROWS), 1)
+    own, other = q_ref[...], p_ref[...]
+    blocks = (jnp.where(lower, own, other), jnp.where(lower, other, own))
+    qg = jnp.concatenate([q[:, a * HEAD : (a + 1) * HEAD] for q in blocks for a in range(4)], axis=0)
+    vis = [place <= query + c * (2 * ROWS) for c in range(2)]
+    scores = nt(kv_ref[:, :, 0:HEAD].reshape(keys, HEAD), qg)
+    scores = jnp.where(jnp.concatenate(vis[:1] * 4 + vis[1:] * 4, axis=1), scores, LOW)
+    peak = jnp.maximum(jnp.max(scores, axis=0, keepdims=True), 0.1 * LOW)
+    if before is not None:
+        peak = jnp.maximum(peak, before[0])
+    w = jnp.exp2((scores - peak) * LOG2)
+    total = jnp.sum(w, axis=0, keepdims=True)
+    summed = tn(kv_ref[:, :, HEAD:].reshape(keys, HEAD), w.astype(bf16))
+    if before is not None:
+        shrink = jnp.exp2((before[0] - peak) * LOG2)
+        total, summed = total + before[1] * shrink, summed + before[2] * shrink
     return peak, total, summed
 
 
-def first_kernel(q_ref, kv_ref, sum_out, stat_out):
-    peak, total, summed = attend(q_ref, kv_ref, lax.rem(lax.axis_index("seq"), 2), None)
+def first_kernel(q_ref, p_ref, kv_ref, sum_out, stat_out):
+    peak, total, summed = attend(q_ref, p_ref, kv_ref, lax.rem(lax.axis_index("seq"), SUPER), None)
     sum_out[...] = summed
-    stat_out[...] = jnp.where(iota((8, 4 * ROWS), 0) == 0, peak, total)
-
-
-def second_kernel(q_ref, kv_ref, sum_ref, stat_ref, out_ref):
+    stat_out[...] = jnp.where(iota((8, TP * ROWS), 0) == 0, peak, total)
+
+
+def second_kernel(q_ref, p_ref, kv_ref, sum_ref, stat_ref, out_ref):
     before = (stat_ref[0:1, :], stat_ref[1:2, :], sum_ref[...])
-    peak, total, summed = attend(q_ref, kv_ref, 1 - lax.rem(lax.axis_index("seq"), 2), before)
-    sub = iota((16, 4 * ROWS), 0)
-    stats = jnp.zeros((16, 4 * ROWS), f32)
-    for k, part in enumerate(cut(peak * SCALE, 3) + cut(total, 3)):
-        stats = jnp.where(sub == k, part, stats)
-    for a in range(4):
+    part = lax.rem(lax.axis_index("seq"), SUPER)
+    part = part + 1 - 2 * lax.rem(part, 2)
+    peak, total, summed = attend(q_ref, p_ref, kv_ref, part, before)
+    sub = iota((16, TP * ROWS), 0)
+    stats = jnp.zeros((16, TP * ROWS), f32)
+    for k, piece in enumerate(cut(peak * SCALE, 3) + cut(total, 3)):
+        stats = jnp.where(sub == k, piece, stats)
+    for a in range(TP):
         cols = slice(a * ROWS, (a + 1) * ROWS)
         out_ref[a, 0:HEAD, :] = summed[:, cols].astype(bf16)
         out_ref[a, HEAD:, :] = stats[:, cols].astype(bf16)
@@ -247,7 +245,7 @@
 
 def project_kernel(rd_ref, w_ref, p_ref, out_ref):
     peaks, totals = [], []
-    for j in range(TP // 2):
+    for j in range(TP):
         stats = rd_ref[j, HEAD:, :].astype(f32)
         peaks.append(stats[0:1] + stats[1:2] + stats[2:3])
         totals.append(stats[3:4] + stats[4:5] + stats[5:6])
@@ -256,7 +254,7 @@
         peak = jnp.maximum(peak, p)
     total = jnp.zeros((1, ROWS), f32)
     summed = jnp.zeros((HEAD, ROWS), f32)
-    for j in range(TP // 2):
+    for j in range(TP):
         scale = jnp.exp(peaks[j] - peak)
         total = total + totals[j] * scale
         summed = summed + rd_ref[j, 0:HEAD, :].astype(f32) * scale
@@ -326,16 +324,20 @@
         2 * 10**5,
     )
     totals = call(total_kernel, "totals", ((SUPER, 64, STATE), bf16), (ra, keep, got), 10**7, 10**6)
+    q_own = call(pick_kernel, "pick", ((ROWS, QUERY // 2), bf16), (queries, totals), 10**7, 10**6, left=(1,))
+    q_other = lax.ppermute(q_own, "seq", [(i, i ^ 2) for i in range(GROUP * SUPER)])
     rb = swap(totals, "seq", far)
-    enter = call(enter_kernel, "enter", ((GROUP, KV + OWN, STATE), bf16), (ra, rb), 10**7, 10**6)
+    enter = call(
+        enter_kernel, "enter", ((GROUP, KV + OWN, STATE), bf16), (ra, rb, q_other), 10**7, 10**6, left=(2,)
+    )
     rc = swap(enter, "seq", near)
     own = rc[:, :KV, :]
     other = lax.ppermute(own, "seq", [(i, i ^ 1) for i in range(GROUP * SUPER)])
     summed, stats = call(
         first_kernel,
         "attend_own",
-        [((HEAD, 4 * ROWS), f32), ((8, 4 * ROWS), f32)],
-        (queries, own),
+        [((HEAD, TP * ROWS), f32), ((8, TP * ROWS), f32)],
+        (q_own, q_other, own),
         3 * 10**8,
         2 * 10**6,
         5 * 10**5,
@@ -343,13 +345,13 @@
     partial = call(
         second_kernel,
         "attend_other",
-        ((TP // 2, HEAD + 16, ROWS), bf16),
-        (queries, other, summed, stats),
+        ((TP, HEAD + 16, ROWS), bf16),
+        (q_own, q_other, other, summed, stats),
         3 * 10**8,
         2 * 10**6,
         5 * 10**5,
     )
-    rd = swap(partial, "tp", row)
+    rd = swap(partial, ("seq", "tp"), heads)
     ssm = call(
         carry_kernel, "carry", ((ROWS, D), f32), (rc, read, ya, yb, w_ssm, partial), 10**9, 10**7, left=(5,)
     )

time: 103 us -> 100 us (0.971)
  blocking collectives: 65 us -> 32.2 us
  waiting for transfers between devices: 7.64 us -> 22.6 us
  starting transfers between devices: 19.4 us -> 33.3 us
    all_to_all x3 -> x2, blocking collectives: 65 us -> 32.2 us  [swap(): return lax.all_to_all(x, axis, 0, 0, axis_index_groups=groups)]
    all_to_all x2 -> x3, starting transfers between devices: 11.8 us -> 24.4 us  [swap(): return lax.all_to_all(x, axis, 0, 0, axis_index_groups=groups)]
    all_to_all x2 -> x3, waiting for transfers between devices: 4.62 us -> 14.8 us  [swap(): return lax.all_to_all(x, axis, 0, 0, axis_index_groups=groups)]
    ppermute x0 -> x1, waiting for transfers between devices: none -> 4.94 us  [local(): lax.ppermute(q_own, 'seq', [(i, i ^ 2) for i in range(GROUP * SUPER)])]
    ppermute x0 -> x1, starting transfers between devices: none -> 1.92 us  [local(): lax.ppermute(q_own, 'seq', [(i, i ^ 2) for i in range(GROUP * SUPER)])]
    pallas_call x9 -> x10, Pallas kernels: 8.02 us -> 8.78 us  [call(): pl.pallas_call(kernel, name=name, out_shape=shapes if many else shapes[0]...]
  transfers between devices with their start and end apart: 4 -> 6, of which waited for: 4 -> 6; matrix products, arithmetic and copies ran while one was open for 0% -> 0% of each run, Pallas kernels for 2% -> 2%
where the time goes in v3:
time: 100 us; the launch traced here: 98.5 us
  starting transfers between devices  33.3 us (33%)
  blocking collectives  32.2 us (32%)
  waiting for transfers between devices  22.6 us (23%)
  Pallas kernels  8.78 us (9%)
  local copies, waits for them, and re-layouts  1.46 us (1%)
    all_to_all x2, blocking collectives, swap(): return lax.all_to_all(x, axis, 0, 0, axis_index_groups=groups)  32.2 us
    all_to_all x3, starting transfers between devices, swap(): return lax.all_to_all(x, axis, 0, 0, axis_index_groups=groups)  24.4 us
    all_to_all x3, waiting for transfers between devices, swap(): return lax.all_to_all(x, axis, 0, 0, axis_index_groups=groups)  14.8 us
    pallas_call x10, Pallas kernels, call(): pl.pallas_call(kernel, name=name, out_shape=shapes if many else shapes[0]...  8.78 us
    ppermute x1, waiting for transfers between devices, local(): lax.ppermute(q_own, 'seq', [(i, i ^ 2) for i in range(GROUP * SUPER)])  4.94 us
    ppermute x1, starting transfers between devices, local(): got = lax.ppermute(give, 'tp', [(i, i ^ 4) for i in range(TP)])  4.81 us
    ppermute x1, waiting for transfers between devices, local(): got = lax.ppermute(give, 'tp', [(i, i ^ 4) for i in range(TP)])  2.55 us
    ppermute x1, starting transfers between devices, local(): other = lax.ppermute(own, 'seq', [(i, i ^ 1) for i in range(GROUP * SUPER)])  2.15 us
  transfers between devices with their start and end apart: 6, of which 6 were waited for; matrix products, arithmetic and copies ran while one was open for 0% of the time, Pallas kernels for 2%

profile of v3, /device:TPU:6, one launch (start us, length us, event | category | flops | bytes accessed | tf_op | source)
XLA Modules:
  0.0 98.5 jit_solution(9327442411541636674)
XLA Ops:
  0.0 2.6 %states.1 = (bf16[16,32,256]{2,1,0:T(8,128)(2,1)}, bf16[16,256]{1,0:T(8,128)(2,1)}, bf16[16,256]{1,0:T(8,128)(2,1)}) custom-call(bf16[128,384]{1,0:T(8,128)(2,1)} %x_ref.1, bf16[128,256]{1,0:T(8,128)(2,1)} %b_ref.1, f32[6,128]{1,0:T(8,128)} %bitcast.1, bf16[16,256]{1,0:T(8,128)(2,1)} %k_hbm.1, bf16[16,256]{1,0:T(8,128)(2,1)} %v_hbm.1), custom_call_target="tpu_custom_call" | custom-call | flops 100000000 | bytes 1000000 | tf_op jit(solution)/shard_map/states/pallas_call | solution.py:279
  2.6 7.0 %all-to-all-start = ((bf16[16,32,256]{2,1,0:T(8,128)(2,1)}), bf16[16,32,256]{2,1,0:T(8,128)(2,1)S(1)}, u32[]{:S(2)}, u32[]{:S(2)}) async-start(bf16[16,32,256]{2,1,0:T(8,128)(2,1)} %get-tuple-element.12), calls=%async_computation | async-start | bytes 524288 | tf_op jit(solution)/shard_map/all_to_all | solution.py:292
  9.6 4.8 %collective-permute-start = (bf16[16,256]{1,0:T(8,128)(2,1)}, bf16[16,256]{1,0:T(8,128)(2,1)S(1)}, u32[]{:S(2)}, u32[]{:S(2)}) collective-permute-start(bf16[16,256]{1,0:T(8,128)(2,1)} %get-tuple-element.14), channel_id=1, source_target_pairs={{0,4},{1,5},{2,6},{3,7},{4,0},{5,1},{6,2},{7,3},{8,12},{9,13},{10,... | collective-permute-start | bytes 24584 | tf_op jit(solution)/shard_map/ppermute | solution.py:316
  14.4 2.5 %collective-permute-done.got_ref = bf16[16,256]{1,0:T(8,128)(2,1)S(1)} collective-permute-done((bf16[16,256]{1,0:T(8,128)(2,1)}, bf16[16,256]{1,0:T(8,128)(2,1)S(1)}, u32[]{:S(2)}, u32[]{:S(2)}) %collective-permute-start) | collective-permute-done | bytes 8224 | tf_op jit(solution)/shard_map/ppermute | solution.py:316
  17.0 2.7 %all-to-all-done.ra_ref = bf16[16,32,256]{2,1,0:T(8,128)(2,1)S(1)} async-done(((bf16[16,32,256]{2,1,0:T(8,128)(2,1)}), bf16[16,32,256]{2,1,0:T(8,128)(2,1)S(1)}, u32[]{:S(2)}, u32[]{:S(2)}) %all-to-all-start) | async-done | bytes 262176 | tf_op jit(solution)/shard_map/all_to_all | solution.py:292
  19.6 0.7 copy-done.4
  20.3 0.8 totals.1.after_ref
  21.1 12.4 %all-to-all-start.1 = ((bf16[4,64,256]{2,1,0:T(8,128)(2,1)}), bf16[4,64,256]{2,1,0:T(8,128)(2,1)S(1)}, u32[]{:S(2)}, u32[]{:S(2)}) async-start(bf16[4,64,256]{2,1,0:T(8,128)(2,1)} %totals.1.after_ref), calls=%async_computation.1 | async-start | bytes 262144 | tf_op jit(solution)/shard_map/all_to_all | solution.py:292
  33.5 1.9 %collective-permute-start.1 = (bf16[128,512]{1,0:T(8,128)(2,1)S(1)}, bf16[128,512]{1,0:T(8,128)(2,1)S(1)}, u32[]{:S(2)}, u32[]{:S(2)}) collective-permute-start(bf16[128,512]{1,0:T(8,128)(2,1)S(1)} %pick.1.q_ref), channel_id=1, source_target_pairs={{0,16},{8,24},{16,0},{24,8},{32,48},{40,56},{48,32},{56,40},{64,80... | collective-permute-start | bytes 393224 | tf_op jit(solution)/shard_map/ppermute | solution.py:328
  35.5 4.9 %collective-permute-done.1.after_ref.p_ref = bf16[128,512]{1,0:T(8,128)(2,1)S(1)} collective-permute-done((bf16[128,512]{1,0:T(8,128)(2,1)S(1)}, bf16[128,512]{1,0:T(8,128)(2,1)S(1)}, u32[]{:S(2)}, u32[]{:S(2)}) %collective-permute-start.1) | collective-permute-done | bytes 131104 | tf_op jit(solution)/shard_map/ppermute | solution.py:328
  40.4 8.2 %all-to-all-done.1.rb_ref = bf16[4,64,256]{2,1,0:T(8,128)(2,1)S(1)} async-done(((bf16[4,64,256]{2,1,0:T(8,128)(2,1)}), bf16[4,64,256]{2,1,0:T(8,128)(2,1)S(1)}, u32[]{:S(2)}, u32[]{:S(2)}) %all-to-all-start.1) | async-done | bytes 131104 | tf_op jit(solution)/shard_map/all_to_all | solution.py:292
  48.6 0.1 enter.1
  48.7 16.2 %all_to_all.25.s_ref = bf16[16,56,256]{2,1,0:T(8,128)(2,1)S(1)} all-to-all(bf16[16,56,256]{2,1,0:T(8,128)(2,1)S(1)} %enter.1), channel_id=1, replica_groups={{0,8,16,24,32,40,48,56,64,72,80,88,96,104,112,120},{128,136,144,152,160..., dimensions={0} | all-to-all | bytes 917504 | tf_op jit(solution)/shard_map/all_to_all | solution.py:292
  65.0 0.0 copy-start.3
  65.0 0.0 copy-start.5
  65.0 0.0 copy-start.6
  65.0 0.0 copy-start.7
  65.0 0.0 copy-start.8
  65.0 2.2 %collective-permute-start.2 = (bf16[16,32,256]{2,1,0:T(8,128)(2,1)S(1)}, bf16[16,32,256]{2,1,0:T(8,128)(2,1)S(1)}, u32[]{:S(2)}, u32[]{:S(2)}) collective-permute-start(bf16[16,32,256]{2,1,0:T(8,128)(2,1)S(1)} %slice.4.kv_ref), channel_id=1, source_target_pairs={{0,8},{8,0},{16,24},{24,16},{32,40},{40,32},{48,56},{56,48},{64,72... | collective-permute-start | bytes 786440 | tf_op jit(solution)/shard_map/ppermute | solution.py:335
  67.2 1.1 %attend_own.1 = (f32[128,1024]{1,0:T(8,128)S(1)}, f32[8,1024]{1,0:T(8,128)S(1)}) custom-call(bf16[128,512]{1,0:T(8,128)(2,1)S(1)} %pick.1.q_ref, bf16[128,512]{1,0:T(8,128)(2,1)S(1)} %collective-permute-done.1.after_ref.p_ref, bf16[16,32,256]{2,1,0:T(8,128)(2,1)S(1)} %slice.4.kv_ref), custom_call_target="tpu_custom_call" | custom-call | flops 300000000 | bytes 2000000 | tf_op jit(solution)/shard_map/attend_own/pallas_call | solution.py:279
  68.3 0.3 collective-permute-done.2.kv_ref
  68.6 1.8 %attend_other.1.after_ref = bf16[8,144,128]{2,1,0:T(8,128)(2,1)} custom-call(bf16[128,512]{1,0:T(8,128)(2,1)S(1)} %pick.1.q_ref, bf16[128,512]{1,0:T(8,128)(2,1)S(1)} %collective-permute-done.1.after_ref.p_ref, bf16[16,32,256]{2,1,0:T(8,128)(2,1)S(1)} %collective-permute-done.2.kv_ref, f32[128,1024]{1,0:T(8,128)S(1)} %get-tuple-element.15.sum_ref, ...), custom_call_target="tpu_custom_call" | custom-call | flops 300000000 | bytes 2000000 | tf_op jit(solution)/shard_map/attend_other/pallas_call | solution.py:279
  70.4 5.0 %all-to-all-start.3 = ((bf16[8,144,128]{2,1,0:T(8,128)(2,1)}), bf16[8,144,128]{2,1,0:T(8,128)(2,1)S(1)}, u32[]{:S(2)}, u32[]{:S(2)}) async-start(bf16[8,144,128]{2,1,0:T(8,128)(2,1)} %attend_other.1.after_ref), calls=%async_computation.3 | async-start | bytes 589824 | tf_op jit(solution)/shard_map/all_to_all | solution.py:292
  75.4 0.0 copy-start
  75.5 0.7 within.1
  76.2 0.7 copy-done
  76.9 0.6 carry.1.p_ref
  77.5 3.9 %all-to-all-done.3.rd_ref = bf16[8,144,128]{2,1,0:T(8,128)(2,1)S(1)} async-done(((bf16[8,144,128]{2,1,0:T(8,128)(2,1)}), bf16[8,144,128]{2,1,0:T(8,128)(2,1)S(1)}, u32[]{:S(2)}, u32[]{:S(2)}) %all-to-all-start.3) | async-done | bytes 294944 | tf_op jit(solution)/shard_map/all_to_all | solution.py:292
  81.4 0.0 copy-done.1
  81.4 0.4 project.1
  81.8 16.0 %all_to_all.26.re_ref = bf16[8,16,2048]{2,1,0:T(8,128)(2,1)S(1)} all-to-all(bf16[8,16,2048]{2,1,0:T(8,128)(2,1)S(1)} %project.1), channel_id=1, replica_groups=mesh['seq'=64,'tp'=8] {'tp'}, dimensions={0} | all-to-all | bytes 1048576 | tf_op jit(solution)/shard_map/all_to_all | solution.py:292
  97.8 0.7 total.1
  (11 shorter events, 0.1 us)
Async XLA Ops:
  0.0 33.5 %copy-start.2 = (bf16[128,1024]{1,0:T(8,128)(2,1)S(1)}, bf16[128,1024]{1,0:T(8,128)(2,1)}, u32[]{:S(2)}) copy-start(bf16[128,1024]{1,0:T(8,128)(2,1)} %q_ref.1) | copy-start | bytes 786436
  2.6 17.1 %all-to-all-start = ((bf16[16,32,256]{2,1,0:T(8,128)(2,1)}), bf16[16,32,256]{2,1,0:T(8,128)(2,1)S(1)}, u32[]{:S(2)}, u32[]{:S(2)}) async-start(bf16[16,32,256]{2,1,0:T(8,128)(2,1)} %get-tuple-element.12), calls=%async_computation | async-start | bytes 524288 | tf_op jit(solution)/shard_map/all_to_all | solution.py:292
  9.6 7.4 %collective-permute-start = (bf16[16,256]{1,0:T(8,128)(2,1)}, bf16[16,256]{1,0:T(8,128)(2,1)S(1)}, u32[]{:S(2)}, u32[]{:S(2)}) collective-permute-start(bf16[16,256]{1,0:T(8,128)(2,1)} %get-tuple-element.14), channel_id=1, source_target_pairs={{0,4},{1,5},{2,6},{3,7},{4,0},{5,1},{6,2},{7,3},{8,12},{9,13},{10,... | collective-permute-start | bytes 24584 | tf_op jit(solution)/shard_map/ppermute | solution.py:316
  19.6 0.7 copy-start.4
  21.1 27.5 %all-to-all-start.1 = ((bf16[4,64,256]{2,1,0:T(8,128)(2,1)}), bf16[4,64,256]{2,1,0:T(8,128)(2,1)S(1)}, u32[]{:S(2)}, u32[]{:S(2)}) async-start(bf16[4,64,256]{2,1,0:T(8,128)(2,1)} %totals.1.after_ref), calls=%async_computation.1 | async-start | bytes 262144 | tf_op jit(solution)/shard_map/all_to_all | solution.py:292
  33.5 6.9 %collective-permute-start.1 = (bf16[128,512]{1,0:T(8,128)(2,1)S(1)}, bf16[128,512]{1,0:T(8,128)(2,1)S(1)}, u32[]{:S(2)}, u32[]{:S(2)}) collective-permute-start(bf16[128,512]{1,0:T(8,128)(2,1)S(1)} %pick.1.q_ref), channel_id=1, source_target_pairs={{0,16},{8,24},{16,0},{24,8},{32,48},{40,56},{48,32},{56,40},{64,80... | collective-permute-start | bytes 393224 | tf_op jit(solution)/shard_map/ppermute | solution.py:328
  65.0 10.4 %copy-start.3 = (bf16[128,256]{1,0:T(8,128)(2,1)S(1)}, bf16[128,256]{1,0:T(8,128)(2,1)}, u32[]{:S(2)}) copy-start(bf16[128,256]{1,0:T(8,128)(2,1)} %c_ref.3) | copy-start | bytes 196612
  65.0 10.4 %copy-start.5 = (bf16[128,384]{1,0:T(8,128)(2,1)S(1)}, bf16[128,384]{1,0:T(8,128)(2,1)}, u32[]{:S(2)}) copy-start(bf16[128,384]{1,0:T(8,128)(2,1)} %x_ref.1) | copy-start | bytes 294916
  65.0 10.4 %copy-start.6 = (bf16[128,384]{1,0:T(8,128)(2,1)S(1)}, bf16[128,384]{1,0:T(8,128)(2,1)}, u32[]{:S(2)}) copy-start(bf16[128,384]{1,0:T(8,128)(2,1)} %g_ref.1) | copy-start | bytes 294916
  65.0 10.4 %copy-start.7 = (bf16[128,256]{1,0:T(8,128)(2,1)S(1)}, bf16[128,256]{1,0:T(8,128)(2,1)}, u32[]{:S(2)}) copy-start(bf16[128,256]{1,0:T(8,128)(2,1)} %b_ref.1) | copy-start | bytes 196612
  65.0 10.4 %copy-start.8 = (f32[128,6]{0,1:T(8,128)S(1)}, f32[128,6]{0,1:T(8,128)}, u32[]{:S(2)}) copy-start(f32[128,6]{0,1:T(8,128)} %param.17) | copy-start | bytes 9220
  65.0 3.6 %collective-permute-start.2 = (bf16[16,32,256]{2,1,0:T(8,128)(2,1)S(1)}, bf16[16,32,256]{2,1,0:T(8,128)(2,1)S(1)}, u32[]{:S(2)}, u32[]{:S(2)}) collective-permute-start(bf16[16,32,256]{2,1,0:T(8,128)(2,1)S(1)} %slice.4.kv_ref), channel_id=1, source_target_pairs={{0,8},{8,0},{16,24},{24,16},{32,40},{40,32},{48,56},{56,48},{64,72... | collective-permute-start | bytes 786440 | tf_op jit(solution)/shard_map/ppermute | solution.py:335
  70.4 11.0 %all-to-all-start.3 = ((bf16[8,144,128]{2,1,0:T(8,128)(2,1)}), bf16[8,144,128]{2,1,0:T(8,128)(2,1)S(1)}, u32[]{:S(2)}, u32[]{:S(2)}) async-start(bf16[8,144,128]{2,1,0:T(8,128)(2,1)} %attend_other.1.after_ref), calls=%async_computation.3 | async-start | bytes 589824 | tf_op jit(solution)/shard_map/all_to_all | solution.py:292
  75.4 1.4 %copy-start = (bf16[384,2048]{1,0:T(8,128)(2,1)S(1)}, bf16[384,2048]{1,0:T(8,128)(2,1)}, u32[]{:S(2)}) copy-start(bf16[384,2048]{1,0:T(8,128)(2,1)} %w_ref.2) | copy-start | bytes 4718596
  76.9 4.5 %copy-start.1 = (bf16[128,2048]{1,0:T(8,128)(2,1)S(1)}, bf16[128,2048]{1,0:T(8,128)(2,1)}, u32[]{:S(2)}) copy-start(bf16[128,2048]{1,0:T(8,128)(2,1)} %w_ref.3) | copy-start | bytes 1572868

commit v4 on v3

--- a/solution.py
+++ b/solution.py
@@ -76,7 +76,7 @@
 
 
 def states_kernel(
-    x_hbm, b_hbm, r_hbm, k_hbm, v_hbm, out_ref, keep_ref, give_ref, x_ref, b_ref, r_ref, k_ref, v_ref, sems
+    x_hbm, b_hbm, r_hbm, k_hbm, v_hbm, out_ref, give_ref, x_ref, b_ref, r_ref, k_ref, v_ref, sems
 ):
     copies = [
         pltpu.make_async_copy(source, target, sems.at[k])
@@ -86,21 +86,15 @@
     ]
     for copy in copies:
         copy.start()
-    for copy in copies:
-        copy.wait()
-    first = lax.axis_index("tp") < TP // 2
-    kv = [
-        jnp.concatenate([k_ref[:, HEAD * g : HEAD * (g + 1)], v_ref[:, HEAD * g : HEAD * (g + 1)]], axis=1)
-        for g in range(2)
-    ]
-    keep_ref[...] = jnp.where(first, kv[0], kv[1])
-    give_ref[...] = jnp.where(first, kv[1], kv[0])
+    copies[0].wait()
     rates = by_token(r_ref[...])
     later = (iota((ROWS, ROWS), 1) > iota((ROWS, ROWS), 0)).astype(bf16)
-    rx = spread(rates, (ROWS, CH), 1, HDIM)
-    after = sum(nn(later, part.astype(bf16)) for part in cut(rx, 3))
-    xs = x_ref[...].astype(f32) * jnp.exp(-after)
+    after = sum(nn(later, part.astype(bf16)) for part in cut(rates, 3))
+    left = jnp.exp(-spread(after, (ROWS, CH), 1, HDIM))
+    copies[1].wait()
+    xs = x_ref[...].astype(f32) * left
     hi, lo = cut(xs.T, 2)
+    copies[2].wait()
     b = b_ref[...]
     state = nn(hi.astype(bf16), b) + nn(lo.astype(bf16), b)
     total = jnp.exp(-jnp.sum(rates, axis=0, keepdims=True))
@@ -114,6 +108,14 @@
     fac = jnp.where(sub == 0, hi, jnp.where(sub == 1, lo, 0.0))
     fac = jnp.where(iota(shape, 2) < OWN, fac, 0.0)
     out_ref[...] = jnp.concatenate([state.reshape(GROUP, OWN, STATE), fac], axis=1).astype(bf16)
+    copies[3].wait()
+    copies[4].wait()
+    first = lax.axis_index("tp") < TP // 2
+    kv = [
+        jnp.concatenate([k_ref[:, HEAD * g : HEAD * (g + 1)], v_ref[:, HEAD * g : HEAD * (g + 1)]], axis=1)
+        for g in range(2)
+    ]
+    give_ref[...] = jnp.where(first, kv[1], kv[0])
 
 
 def unpack(block):
@@ -130,6 +132,12 @@
     hi, lo = cut(row, 2)
     sub = iota((8, STATE), 0)
     return jnp.where(sub == 0, hi, jnp.where(sub == 1, lo, 0.0))
+
+
+def keep_kernel(k_ref, v_ref, out_ref):
+    first = lax.axis_index("tp") < TP // 2
+    for c, ref in enumerate((k_ref, v_ref)):
+        out_ref[:, HEAD * c : HEAD * (c + 1)] = jnp.where(first, ref[:, :HEAD], ref[:, HEAD:])
 
 
 def total_kernel(ra_ref, keep_ref, got_ref, out_ref):
@@ -294,10 +302,10 @@
 
 def local(queries, keys, values, x, gate, write, read, rates, w_attn, w_ssm):
     rates = rates.T
-    sent, keep, give = call(
+    sent, give = call(
         states_kernel,
         "states",
-        [((GROUP, PAD, STATE), bf16), ((SLICE, 2 * HEAD), bf16), ((SLICE, 2 * HEAD), bf16)],
+        [((GROUP, PAD, STATE), bf16), ((SLICE, 2 * HEAD), bf16)],
         (x, write, rates, keys, values),
         10**8,
         10**6,
@@ -314,6 +322,7 @@
     )
     ra = swap(sent, "seq", near)
     got = lax.ppermute(give, "tp", [(i, i ^ 4) for i in range(TP)])
+    keep = call(keep_kernel, "keep", ((SLICE, 2 * HEAD), bf16), (keys, values), 10**7, 10**6)
     ya, yb = call(
         within_kernel,
         "within",

time: 100 us -> 99.4 us (level)
  waiting for transfers between devices: 22.6 us -> 21.2 us
    ppermute x1, waiting for transfers between devices: 2.55 us -> 1.14 us  [local(): got = lax.ppermute(give, 'tp', [(i, i ^ 4) for i in range(TP)])]
    unnamed x18 -> x20, local copies, waits for them, and re-layouts: 1.44 us -> 2.13 us
    pallas_call x10 -> x11, Pallas kernels: 8.78 us -> 8.64 us  [call(): pl.pallas_call(kernel, name=name, out_shape=shapes if many else shapes[0]...]
where the time goes in v4:
time: 99.4 us; the launch traced here: 97.6 us
  starting transfers between devices  33.3 us (34%)
  blocking collectives  32.2 us (32%)
  waiting for transfers between devices  21.2 us (21%)
  Pallas kernels  8.64 us (9%)
  local copies, waits for them, and re-layouts  2.14 us (2%)
    all_to_all x2, blocking collectives, swap(): return lax.all_to_all(x, axis, 0, 0, axis_index_groups=groups)  32.2 us
    all_to_all x3, starting transfers between devices, swap(): return lax.all_to_all(x, axis, 0, 0, axis_index_groups=groups)  24.4 us
    all_to_all x3, waiting for transfers between devices, swap(): return lax.all_to_all(x, axis, 0, 0, axis_index_groups=groups)  14.8 us
    pallas_call x11, Pallas kernels, call(): pl.pallas_call(kernel, name=name, out_shape=shapes if many else shapes[0]...  8.64 us
    ppermute x1, waiting for transfers between devices, local(): lax.ppermute(q_own, 'seq', [(i, i ^ 2) for i in range(GROUP * SUPER)])  4.94 us
    ppermute x1, starting transfers between devices, local(): got = lax.ppermute(give, 'tp', [(i, i ^ 4) for i in range(TP)])  4.81 us
    ppermute x1, starting transfers between devices, local(): other = lax.ppermute(own, 'seq', [(i, i ^ 1) for i in range(GROUP * SUPER)])  2.15 us
    unnamed x20, local copies, waits for them, and re-layouts  2.13 us
  transfers between devices with their start and end apart: 6, of which 6 were waited for; matrix products, arithmetic and copies ran while one was open for 0% of the time, Pallas kernels for 2%

profile of v4, /device:TPU:6, one launch (start us, length us, event | category | flops | bytes accessed | tf_op | source)
XLA Modules:
  0.0 97.6 jit_solution(8580282692445401452)
XLA Ops:
  0.0 2.4 %states.1 = (bf16[16,32,256]{2,1,0:T(8,128)(2,1)}, bf16[16,256]{1,0:T(8,128)(2,1)}) custom-call(bf16[128,384]{1,0:T(8,128)(2,1)} %x_ref.1, bf16[128,256]{1,0:T(8,128)(2,1)} %b_ref.1, f32[6,128]{1,0:T(8,128)} %bitcast.1, bf16[16,256]{1,0:T(8,128)(2,1)} %k_ref.1, bf16[16,256]{1,0:T(8,128)(2,1)} %v_ref.1), custom_call_target="tpu_custom_call" | custom-call | flops 100000000 | bytes 1000000 | tf_op jit(solution)/shard_map/states/pallas_call | solution.py:287
  2.4 7.0 %all-to-all-start = ((bf16[16,32,256]{2,1,0:T(8,128)(2,1)}), bf16[16,32,256]{2,1,0:T(8,128)(2,1)S(1)}, u32[]{:S(2)}, u32[]{:S(2)}) async-start(bf16[16,32,256]{2,1,0:T(8,128)(2,1)} %get-tuple-element.11), calls=%async_computation | async-start | bytes 524288 | tf_op jit(solution)/shard_map/all_to_all | solution.py:300
  9.4 4.8 %collective-permute-start = (bf16[16,256]{1,0:T(8,128)(2,1)}, bf16[16,256]{1,0:T(8,128)(2,1)S(1)}, u32[]{:S(2)}, u32[]{:S(2)}) collective-permute-start(bf16[16,256]{1,0:T(8,128)(2,1)} %get-tuple-element.12), channel_id=1, source_target_pairs={{0,4},{1,5},{2,6},{3,7},{4,0},{5,1},{6,2},{7,3},{8,12},{9,13},{10,... | collective-permute-start | bytes 24584 | tf_op jit(solution)/shard_map/ppermute | solution.py:324
  14.3 0.0 copy-start.7
  14.3 0.7 copy-done.7
  15.0 0.7 copy-done.8
  15.7 1.1 %collective-permute-done.got_ref = bf16[16,256]{1,0:T(8,128)(2,1)S(1)} collective-permute-done((bf16[16,256]{1,0:T(8,128)(2,1)}, bf16[16,256]{1,0:T(8,128)(2,1)S(1)}, u32[]{:S(2)}, u32[]{:S(2)}) %collective-permute-start) | collective-permute-done | bytes 8224 | tf_op jit(solution)/shard_map/ppermute | solution.py:324
  16.8 2.7 %all-to-all-done.ra_ref = bf16[16,32,256]{2,1,0:T(8,128)(2,1)S(1)} async-done(((bf16[16,32,256]{2,1,0:T(8,128)(2,1)}), bf16[16,32,256]{2,1,0:T(8,128)(2,1)S(1)}, u32[]{:S(2)}, u32[]{:S(2)}) %all-to-all-start) | async-done | bytes 262176 | tf_op jit(solution)/shard_map/all_to_all | solution.py:300
  19.5 0.8 totals.1.after_ref
  20.3 12.4 %all-to-all-start.1 = ((bf16[4,64,256]{2,1,0:T(8,128)(2,1)}), bf16[4,64,256]{2,1,0:T(8,128)(2,1)S(1)}, u32[]{:S(2)}, u32[]{:S(2)}) async-start(bf16[4,64,256]{2,1,0:T(8,128)(2,1)} %totals.1.after_ref), calls=%async_computation.1 | async-start | bytes 262144 | tf_op jit(solution)/shard_map/all_to_all | solution.py:300
  32.7 1.9 %collective-permute-start.1 = (bf16[128,512]{1,0:T(8,128)(2,1)S(1)}, bf16[128,512]{1,0:T(8,128)(2,1)S(1)}, u32[]{:S(2)}, u32[]{:S(2)}) collective-permute-start(bf16[128,512]{1,0:T(8,128)(2,1)S(1)} %pick.1.q_ref), channel_id=1, source_target_pairs={{0,16},{8,24},{16,0},{24,8},{32,48},{40,56},{48,32},{56,40},{64,80... | collective-permute-start | bytes 393224 | tf_op jit(solution)/shard_map/ppermute | solution.py:337
  34.6 4.9 %collective-permute-done.1.after_ref.p_ref = bf16[128,512]{1,0:T(8,128)(2,1)S(1)} collective-permute-done((bf16[128,512]{1,0:T(8,128)(2,1)S(1)}, bf16[128,512]{1,0:T(8,128)(2,1)S(1)}, u32[]{:S(2)}, u32[]{:S(2)}) %collective-permute-start.1) | collective-permute-done | bytes 131104 | tf_op jit(solution)/shard_map/ppermute | solution.py:337
  39.6 8.2 %all-to-all-done.1.rb_ref = bf16[4,64,256]{2,1,0:T(8,128)(2,1)S(1)} async-done(((bf16[4,64,256]{2,1,0:T(8,128)(2,1)}), bf16[4,64,256]{2,1,0:T(8,128)(2,1)S(1)}, u32[]{:S(2)}, u32[]{:S(2)}) %all-to-all-start.1) | async-done | bytes 131104 | tf_op jit(solution)/shard_map/all_to_all | solution.py:300
  47.7 0.1 enter.1
  47.9 16.2 %all_to_all.25.s_ref = bf16[16,56,256]{2,1,0:T(8,128)(2,1)S(1)} all-to-all(bf16[16,56,256]{2,1,0:T(8,128)(2,1)S(1)} %enter.1), channel_id=1, replica_groups={{0,8,16,24,32,40,48,56,64,72,80,88,96,104,112,120},{128,136,144,152,160..., dimensions={0} | all-to-all | bytes 917504 | tf_op jit(solution)/shard_map/all_to_all | solution.py:300
  64.1 0.0 copy-start.3
  64.1 0.0 copy-start.4
  64.2 0.0 copy-start.6
  64.2 0.0 copy-start.9
  64.2 2.2 %collective-permute-start.2 = (bf16[16,32,256]{2,1,0:T(8,128)(2,1)S(1)}, bf16[16,32,256]{2,1,0:T(8,128)(2,1)S(1)}, u32[]{:S(2)}, u32[]{:S(2)}) collective-permute-start(bf16[16,32,256]{2,1,0:T(8,128)(2,1)S(1)} %slice.4.kv_ref), channel_id=1, source_target_pairs={{0,8},{8,0},{16,24},{24,16},{32,40},{40,32},{48,56},{56,48},{64,72... | collective-permute-start | bytes 786440 | tf_op jit(solution)/shard_map/ppermute | solution.py:344
  66.3 1.1 %attend_own.1 = (f32[128,1024]{1,0:T(8,128)S(1)}, f32[8,1024]{1,0:T(8,128)S(1)}) custom-call(bf16[128,512]{1,0:T(8,128)(2,1)S(1)} %pick.1.q_ref, bf16[128,512]{1,0:T(8,128)(2,1)S(1)} %collective-permute-done.1.after_ref.p_ref, bf16[16,32,256]{2,1,0:T(8,128)(2,1)S(1)} %slice.4.kv_ref), custom_call_target="tpu_custom_call" | custom-call | flops 300000000 | bytes 2000000 | tf_op jit(solution)/shard_map/attend_own/pallas_call | solution.py:287
  67.4 0.3 collective-permute-done.2.kv_ref
  67.7 1.8 %attend_other.1.after_ref = bf16[8,144,128]{2,1,0:T(8,128)(2,1)} custom-call(bf16[128,512]{1,0:T(8,128)(2,1)S(1)} %pick.1.q_ref, bf16[128,512]{1,0:T(8,128)(2,1)S(1)} %collective-permute-done.1.after_ref.p_ref, bf16[16,32,256]{2,1,0:T(8,128)(2,1)S(1)} %collective-permute-done.2.kv_ref, f32[128,1024]{1,0:T(8,128)S(1)} %get-tuple-element.13.sum_ref, ...), custom_call_target="tpu_custom_call" | custom-call | flops 300000000 | bytes 2000000 | tf_op jit(solution)/shard_map/attend_other/pallas_call | solution.py:287
  69.6 5.0 %all-to-all-start.3 = ((bf16[8,144,128]{2,1,0:T(8,128)(2,1)}), bf16[8,144,128]{2,1,0:T(8,128)(2,1)S(1)}, u32[]{:S(2)}, u32[]{:S(2)}) async-start(bf16[8,144,128]{2,1,0:T(8,128)(2,1)} %attend_other.1.after_ref), calls=%async_computation.3 | async-start | bytes 589824 | tf_op jit(solution)/shard_map/all_to_all | solution.py:300
  74.6 0.0 copy-start
  74.6 0.7 within.1
  75.3 0.7 copy-done
  76.0 0.6 carry.1.p_ref
  76.6 3.9 %all-to-all-done.3.rd_ref = bf16[8,144,128]{2,1,0:T(8,128)(2,1)S(1)} async-done(((bf16[8,144,128]{2,1,0:T(8,128)(2,1)}), bf16[8,144,128]{2,1,0:T(8,128)(2,1)S(1)}, u32[]{:S(2)}, u32[]{:S(2)}) %all-to-all-start.3) | async-done | bytes 294944 | tf_op jit(solution)/shard_map/all_to_all | solution.py:300
  80.5 0.4 project.1
  80.9 16.0 %all_to_all.26.re_ref = bf16[8,16,2048]{2,1,0:T(8,128)(2,1)S(1)} all-to-all(bf16[8,16,2048]{2,1,0:T(8,128)(2,1)S(1)} %project.1), channel_id=1, replica_groups=mesh['seq'=64,'tp'=8] {'tp'}, dimensions={0} | all-to-all | bytes 1048576 | tf_op jit(solution)/shard_map/all_to_all | solution.py:300
  96.9 0.7 total.1
  (14 shorter events, 0.1 us)
Async XLA Ops:
  0.0 32.7 %copy-start.2 = (bf16[128,1024]{1,0:T(8,128)(2,1)S(1)}, bf16[128,1024]{1,0:T(8,128)(2,1)}, u32[]{:S(2)}) copy-start(bf16[128,1024]{1,0:T(8,128)(2,1)} %q_ref.1) | copy-start | bytes 786436
  2.4 17.1 %all-to-all-start = ((bf16[16,32,256]{2,1,0:T(8,128)(2,1)}), bf16[16,32,256]{2,1,0:T(8,128)(2,1)S(1)}, u32[]{:S(2)}, u32[]{:S(2)}) async-start(bf16[16,32,256]{2,1,0:T(8,128)(2,1)} %get-tuple-element.11), calls=%async_computation | async-start | bytes 524288 | tf_op jit(solution)/shard_map/all_to_all | solution.py:300
  9.4 7.4 %collective-permute-start = (bf16[16,256]{1,0:T(8,128)(2,1)}, bf16[16,256]{1,0:T(8,128)(2,1)S(1)}, u32[]{:S(2)}, u32[]{:S(2)}) collective-permute-start(bf16[16,256]{1,0:T(8,128)(2,1)} %get-tuple-element.12), channel_id=1, source_target_pairs={{0,4},{1,5},{2,6},{3,7},{4,0},{5,1},{6,2},{7,3},{8,12},{9,13},{10,... | collective-permute-start | bytes 24584 | tf_op jit(solution)/shard_map/ppermute | solution.py:324
  14.3 0.7 copy-start.7
  15.0 0.7 copy-start.8
  20.3 27.5 %all-to-all-start.1 = ((bf16[4,64,256]{2,1,0:T(8,128)(2,1)}), bf16[4,64,256]{2,1,0:T(8,128)(2,1)S(1)}, u32[]{:S(2)}, u32[]{:S(2)}) async-start(bf16[4,64,256]{2,1,0:T(8,128)(2,1)} %totals.1.after_ref), calls=%async_computation.1 | async-start | bytes 262144 | tf_op jit(solution)/shard_map/all_to_all | solution.py:300
  32.7 6.9 %collective-permute-start.1 = (bf16[128,512]{1,0:T(8,128)(2,1)S(1)}, bf16[128,512]{1,0:T(8,128)(2,1)S(1)}, u32[]{:S(2)}, u32[]{:S(2)}) collective-permute-start(bf16[128,512]{1,0:T(8,128)(2,1)S(1)} %pick.1.q_ref), channel_id=1, source_target_pairs={{0,16},{8,24},{16,0},{24,8},{32,48},{40,56},{48,32},{56,40},{64,80... | collective-permute-start | bytes 393224 | tf_op jit(solution)/shard_map/ppermute | solution.py:337
  64.1 10.4 %copy-start.3 = (bf16[128,256]{1,0:T(8,128)(2,1)S(1)}, bf16[128,256]{1,0:T(8,128)(2,1)}, u32[]{:S(2)}) copy-start(bf16[128,256]{1,0:T(8,128)(2,1)} %c_ref.3) | copy-start | bytes 196612
  64.1 10.4 %copy-start.4 = (bf16[128,384]{1,0:T(8,128)(2,1)S(1)}, bf16[128,384]{1,0:T(8,128)(2,1)}, u32[]{:S(2)}) copy-start(bf16[128,384]{1,0:T(8,128)(2,1)} %x_ref.1) | copy-start | bytes 294916
  64.1 10.4 %copy-start.5 = (bf16[128,384]{1,0:T(8,128)(2,1)S(1)}, bf16[128,384]{1,0:T(8,128)(2,1)}, u32[]{:S(2)}) copy-start(bf16[128,384]{1,0:T(8,128)(2,1)} %g_ref.1) | copy-start | bytes 294916
  64.2 10.4 %copy-start.6 = (bf16[128,256]{1,0:T(8,128)(2,1)S(1)}, bf16[128,256]{1,0:T(8,128)(2,1)}, u32[]{:S(2)}) copy-start(bf16[128,256]{1,0:T(8,128)(2,1)} %b_ref.1) | copy-start | bytes 196612
  64.2 10.4 %copy-start.9 = (f32[128,6]{0,1:T(8,128)S(1)}, f32[128,6]{0,1:T(8,128)}, u32[]{:S(2)}) copy-start(f32[128,6]{0,1:T(8,128)} %param.17) | copy-start | bytes 9220
  64.2 3.6 %collective-permute-start.2 = (bf16[16,32,256]{2,1,0:T(8,128)(2,1)S(1)}, bf16[16,32,256]{2,1,0:T(8,128)(2,1)S(1)}, u32[]{:S(2)}, u32[]{:S(2)}) collective-permute-start(bf16[16,32,256]{2,1,0:T(8,128)(2,1)S(1)} %slice.4.kv_ref), channel_id=1, source_target_pairs={{0,8},{8,0},{16,24},{24,16},{32,40},{40,32},{48,56},{56,48},{64,72... | collective-permute-start | bytes 786440 | tf_op jit(solution)/shard_map/ppermute | solution.py:344
  69.6 11.0 %all-to-all-start.3 = ((bf16[8,144,128]{2,1,0:T(8,128)(2,1)}), bf16[8,144,128]{2,1,0:T(8,128)(2,1)S(1)}, u32[]{:S(2)}, u32[]{:S(2)}) async-start(bf16[8,144,128]{2,1,0:T(8,128)(2,1)} %attend_other.1.after_ref), calls=%async_computation.3 | async-start | bytes 589824 | tf_op jit(solution)/shard_map/all_to_all | solution.py:300
  74.6 1.4 %copy-start = (bf16[384,2048]{1,0:T(8,128)(2,1)S(1)}, bf16[384,2048]{1,0:T(8,128)(2,1)}, u32[]{:S(2)}) copy-start(bf16[384,2048]{1,0:T(8,128)(2,1)} %w_ref.2) | copy-start | bytes 4718596
  76.0 4.5 %copy-start.1 = (bf16[128,2048]{1,0:T(8,128)(2,1)S(1)}, bf16[128,2048]{1,0:T(8,128)(2,1)}, u32[]{:S(2)}) copy-start(bf16[128,2048]{1,0:T(8,128)(2,1)} %w_ref.3) | copy-start | bytes 1572868

commit v5 on v4

--- a/solution.py
+++ b/solution.py
@@ -26,6 +26,7 @@
 LOW = -1e30
 SCALE = 1.0 / math.sqrt(HEAD)
 LOG2 = SCALE * math.log2(math.e)
+GIVE = SLICE + 2 * ROWS
 KV = 32
 
 near = [[GROUP * h + i for i in range(GROUP)] for h in range(SUPER)]
@@ -76,7 +77,7 @@
 
 
 def states_kernel(
-    x_hbm, b_hbm, r_hbm, k_hbm, v_hbm, out_ref, give_ref, x_ref, b_ref, r_ref, k_ref, v_ref, sems
+    x_hbm, b_hbm, r_hbm, k_hbm, v_hbm, q_hbm, out_ref, give_ref, x_ref, b_ref, r_ref, k_ref, v_ref, sems
 ):
     copies = [
         pltpu.make_async_copy(source, target, sems.at[k])
@@ -84,6 +85,11 @@
             [(r_hbm, r_ref), (x_hbm, x_ref), (b_hbm, b_ref), (k_hbm, k_ref), (v_hbm, v_ref)]
         )
     ]
+    first = lax.axis_index("tp") < TP // 2
+    for c in range(2):
+        lanes = pl.ds(pl.multiple_of(jnp.where(first, QUERY // 2, 0) + 2 * HEAD * c, 2 * HEAD), 2 * HEAD)
+        rows = slice(SLICE + ROWS * c, SLICE + ROWS * (c + 1))
+        copies.append(pltpu.make_async_copy(q_hbm.at[:, lanes], give_ref.at[rows], sems.at[5 + c]))
     for copy in copies:
         copy.start()
     copies[0].wait()
@@ -108,14 +114,13 @@
     fac = jnp.where(sub == 0, hi, jnp.where(sub == 1, lo, 0.0))
     fac = jnp.where(iota(shape, 2) < OWN, fac, 0.0)
     out_ref[...] = jnp.concatenate([state.reshape(GROUP, OWN, STATE), fac], axis=1).astype(bf16)
-    copies[3].wait()
-    copies[4].wait()
-    first = lax.axis_index("tp") < TP // 2
+    for copy in copies[3:]:
+        copy.wait()
     kv = [
         jnp.concatenate([k_ref[:, HEAD * g : HEAD * (g + 1)], v_ref[:, HEAD * g : HEAD * (g + 1)]], axis=1)
         for g in range(2)
     ]
-    give_ref[...] = jnp.where(first, kv[1], kv[0])
+    give_ref[0:SLICE, :] = jnp.where(first, kv[1], kv[0])
 
 
 def unpack(block):
@@ -150,16 +155,11 @@
     packed = jnp.concatenate([state, decay_rows(prod)], axis=0).astype(bf16)
     for h in range(SUPER):
         out_ref[h, 0:SLICE, :] = keep_ref[...]
-        out_ref[h, SLICE : 2 * SLICE, :] = got_ref[...]
+        out_ref[h, SLICE : 2 * SLICE, :] = got_ref[0:SLICE, :]
         out_ref[h, 2 * SLICE : 2 * SLICE + PAD, :] = packed
 
 
-def pick_kernel(q_ref, after_ref, out_ref):
-    half = QUERY // 2
-    out_ref[...] = jnp.where(lax.axis_index("tp") < TP // 2, q_ref[:, :half], q_ref[:, half:])
-
-
-def enter_kernel(ra_ref, rb_ref, after_ref, out_ref):
+def enter_kernel(ra_ref, rb_ref, out_ref):
     mine = lax.axis_index("seq") // GROUP
     state = jnp.zeros((OWN, STATE), f32)
     for h in range(SUPER - 1):
@@ -201,12 +201,19 @@
     low_seq = jnp.where(lower, seq, seq - 2)
     keys = GROUP * KV
     n = iota((keys, ROWS), 0)
-    slot = jnp.where(n % KV < SLICE, tp, lax.rem(tp + TP // 2, TP))
-    place = (n // KV) * ROWS + slot * SLICE + n % SLICE + part * (GROUP * ROWS)
+    mine = n % KV < SLICE
+    slot = jnp.where(mine, tp, lax.rem(tp + TP // 2, TP))
+    block = jnp.where(mine, n // KV, (n // KV) ^ 2)
+    place = block * ROWS + slot * SLICE + n % SLICE + part * (GROUP * ROWS)
     query = low_seq * ROWS + iota((keys, ROWS), 1)
-    own, other = q_ref[...], p_ref[...]
-    blocks = (jnp.where(lower, own, other), jnp.where(lower, other, own))
-    qg = jnp.concatenate([q[:, a * HEAD : (a + 1) * HEAD] for q in blocks for a in range(4)], axis=0)
+    first = tp < TP // 2
+    own, other = [], []
+    for a in range(4):
+        own.append(jnp.where(first, q_ref[:, a * HEAD : (a + 1) * HEAD], q_ref[:, (4 + a) * HEAD : (5 + a) * HEAD]))
+        rows = slice(SLICE + ROWS * (a // 2), SLICE + ROWS * (a // 2 + 1))
+        other.append(p_ref[rows, HEAD * (a % 2) : HEAD * (a % 2 + 1)])
+    own, other = jnp.concatenate(own, axis=0), jnp.concatenate(other, axis=0)
+    qg = jnp.concatenate([jnp.where(lower, own, other), jnp.where(lower, other, own)], axis=0)
     vis = [place <= query + c * (2 * ROWS) for c in range(2)]
     scores = nt(kv_ref[:, :, 0:HEAD].reshape(keys, HEAD), qg)
     scores = jnp.where(jnp.concatenate(vis[:1] * 4 + vis[1:] * 4, axis=1), scores, LOW)
@@ -305,11 +312,11 @@
     sent, give = call(
         states_kernel,
         "states",
-        [((GROUP, PAD, STATE), bf16), ((SLICE, 2 * HEAD), bf16)],
-        (x, write, rates, keys, values),
+        [((GROUP, PAD, STATE), bf16), ((GIVE, 2 * HEAD), bf16)],
+        (x, write, rates, keys, values, queries),
         10**8,
         10**6,
-        left=range(5),
+        left=range(6),
         vmem=60,
         scratch=[
             pltpu.VMEM((ROWS, CH), bf16),
@@ -317,11 +324,11 @@
             pltpu.VMEM((HEADS, ROWS), f32),
             pltpu.VMEM((SLICE, 2 * HEAD), bf16),
             pltpu.VMEM((SLICE, 2 * HEAD), bf16),
-            pltpu.SemaphoreType.DMA((5,)),
+            pltpu.SemaphoreType.DMA((7,)),
         ],
     )
     ra = swap(sent, "seq", near)
-    got = lax.ppermute(give, "tp", [(i, i ^ 4) for i in range(TP)])
+    got = lax.ppermute(give, ("seq", "tp"), [(i, i ^ (2 * TP + 4)) for i in range(GROUP * SUPER * TP)])
     keep = call(keep_kernel, "keep", ((SLICE, 2 * HEAD), bf16), (keys, values), 10**7, 10**6)
     ya, yb = call(
         within_kernel,
@@ -333,12 +340,8 @@
         2 * 10**5,
     )
     totals = call(total_kernel, "totals", ((SUPER, 64, STATE), bf16), (ra, keep, got), 10**7, 10**6)
-    q_own = call(pick_kernel, "pick", ((ROWS, QUERY // 2), bf16), (queries, totals), 10**7, 10**6, left=(1,))
-    q_other = lax.ppermute(q_own, "seq", [(i, i ^ 2) for i in range(GROUP * SUPER)])
     rb = swap(totals, "seq", far)
-    enter = call(
-        enter_kernel, "enter", ((GROUP, KV + OWN, STATE), bf16), (ra, rb, q_other), 10**7, 10**6, left=(2,)
-    )
+    enter = call(enter_kernel, "enter", ((GROUP, KV + OWN, STATE), bf16), (ra, rb), 10**7, 10**6)
     rc = swap(enter, "seq", near)
     own = rc[:, :KV, :]
     other = lax.ppermute(own, "seq", [(i, i ^ 1) for i in range(GROUP * SUPER)])
@@ -346,7 +349,7 @@
         first_kernel,
         "attend_own",
         [((HEAD, TP * ROWS), f32), ((8, TP * ROWS), f32)],
-        (q_own, q_other, own),
+        (queries, got, own),
         3 * 10**8,
         2 * 10**6,
         5 * 10**5,
@@ -355,7 +358,7 @@
         second_kernel,
         "attend_other",
         ((TP, HEAD + 16, ROWS), bf16),
-        (q_own, q_other, other, summed, stats),
+        (queries, got, other, summed, stats),
         3 * 10**8,
         2 * 10**6,
         5 * 10**5,

time: 99.4 us -> 99.8 us (level)
  blocking collectives: 32.2 us -> 60.8 us
  waiting for transfers between devices: 21.2 us -> 7.44 us
  starting transfers between devices: 33.3 us -> 19.6 us
    all_to_all x2 -> x3, blocking collectives: 32.2 us -> 60.8 us  [swap(): return lax.all_to_all(x, axis, 0, 0, axis_index_groups=groups)]
    all_to_all x3 -> x2, starting transfers between devices: 24.4 us -> 12 us  [swap(): return lax.all_to_all(x, axis, 0, 0, axis_index_groups=groups)]
    all_to_all x3 -> x2, waiting for transfers between devices: 14.8 us -> 4.36 us  [swap(): return lax.all_to_all(x, axis, 0, 0, axis_index_groups=groups)]
    ppermute x2 -> x1, waiting for transfers between devices: 6.09 us -> 2.78 us  [local(): lax.ppermute(give, ('seq', 'tp'), [(i, i ^ 2 * TP + 4) for i in range(GRO...]
    ppermute x2 -> x1, starting transfers between devices: 6.73 us -> 5.4 us  [local(): lax.ppermute(give, ('seq', 'tp'), [(i, i ^ 2 * TP + 4) for i in range(GRO...]
    pallas_call x11 -> x10, Pallas kernels: 8.64 us -> 8 us  [call(): pl.pallas_call(kernel, name=name, out_shape=shapes if many else shapes[0]...]
  transfers between devices with their start and end apart: 6 -> 4, of which waited for: 6 -> 4; matrix products, arithmetic and copies ran while one was open for 0% -> 0% of each run, Pallas kernels for 2% -> 2%
where the time goes in v5:
time: 99.8 us; the launch traced here: 98.1 us
  blocking collectives  60.8 us (61%)
  starting transfers between devices  19.6 us (20%)
  Pallas kernels  8 us (8%)
  waiting for transfers between devices  7.44 us (7%)
  local copies, waits for them, and re-layouts  2.14 us (2%)
    all_to_all x3, blocking collectives, swap(): return lax.all_to_all(x, axis, 0, 0, axis_index_groups=groups)  60.8 us
    all_to_all x2, starting transfers between devices, swap(): return lax.all_to_all(x, axis, 0, 0, axis_index_groups=groups)  12 us
    pallas_call x10, Pallas kernels, call(): pl.pallas_call(kernel, name=name, out_shape=shapes if many else shapes[0]...  8 us
    ppermute x1, starting transfers between devices, local(): lax.ppermute(give, ('seq', 'tp'), [(i, i ^ 2 * TP + 4) for i in range(GRO...  5.4 us
    all_to_all x2, waiting for transfers between devices, swap(): return lax.all_to_all(x, axis, 0, 0, axis_index_groups=groups)  4.36 us
    ppermute x1, waiting for transfers between devices, local(): lax.ppermute(give, ('seq', 'tp'), [(i, i ^ 2 * TP + 4) for i in range(GRO...  2.78 us
    ppermute x1, starting transfers between devices, local(): other = lax.ppermute(own, 'seq', [(i, i ^ 1) for i in range(GROUP * SUPER)])  2.15 us
    unnamed x20, local copies, waits for them, and re-layouts  2.13 us
  transfers between devices with their start and end apart: 4, of which 4 were waited for; matrix products, arithmetic and copies ran while one was open for 0% of the time, Pallas kernels for 2%

profile of v5, /device:TPU:6, one launch (start us, length us, event | category | flops | bytes accessed | tf_op | source)
XLA Modules:
  0.0 98.1 jit_solution(11195435194042063959)
XLA Ops:
  0.0 2.4 %states.1 = (bf16[16,32,256]{2,1,0:T(8,128)(2,1)}, bf16[272,256]{1,0:T(8,128)(2,1)}) custom-call(bf16[128,384]{1,0:T(8,128)(2,1)} %x_ref.1, bf16[128,256]{1,0:T(8,128)(2,1)} %b_ref.1, f32[6,128]{1,0:T(8,128)} %bitcast.1, bf16[16,256]{1,0:T(8,128)(2,1)} %k_ref.1, bf16[16,256]{1,0:T(8,128)(2,1)} %v_ref.1, bf16[128,1024]{1,0:T(8,128)(2,1)} %q_ref.3), custom_call_target="tpu_custom_call" | custom-call | flops 100000000 | bytes 1000000 | tf_op jit(solution)/shard_map/states/pallas_call | solution.py:294
  2.4 7.0 %all-to-all-start = ((bf16[16,32,256]{2,1,0:T(8,128)(2,1)}), bf16[16,32,256]{2,1,0:T(8,128)(2,1)S(1)}, u32[]{:S(2)}, u32[]{:S(2)}) async-start(bf16[16,32,256]{2,1,0:T(8,128)(2,1)} %get-tuple-element.12), calls=%async_computation | async-start | bytes 524288 | tf_op jit(solution)/shard_map/all_to_all | solution.py:307
  9.5 0.0 copy-start.1
  9.5 5.4 %collective-permute-start = (bf16[272,256]{1,0:T(8,128)(2,1)}, bf16[272,256]{1,0:T(8,128)(2,1)S(1)}, u32[]{:S(2)}, u32[]{:S(2)}) collective-permute-start(bf16[272,256]{1,0:T(8,128)(2,1)} %get-tuple-element.11), channel_id=1, source_target_pairs={{0,20},{1,21},{2,22},{3,23},{4,16},{5,17},{6,18},{7,19},{8,28},{9,... | collective-permute-start | bytes 417800 | tf_op jit(solution)/shard_map/ppermute | solution.py:331
  14.9 0.0 copy-start.6
  14.9 0.7 copy-done.6
  15.6 0.7 copy-done.7
  16.3 2.8 %collective-permute-done.got_ref.p_ref = bf16[272,256]{1,0:T(8,128)(2,1)S(1)} collective-permute-done((bf16[272,256]{1,0:T(8,128)(2,1)}, bf16[272,256]{1,0:T(8,128)(2,1)S(1)}, u32[]{:S(2)}, u32[]{:S(2)}) %collective-permute-start) | collective-permute-done | bytes 139296 | tf_op jit(solution)/shard_map/ppermute | solution.py:331
  19.1 0.4 all-to-all-done.ra_ref
  19.5 0.1 totals.1
  19.6 26.7 %all_to_all.25.rb_ref = bf16[4,64,256]{2,1,0:T(8,128)(2,1)S(1)} all-to-all(bf16[4,64,256]{2,1,0:T(8,128)(2,1)S(1)} %totals.1), channel_id=1, replica_groups={{0,128,256,384},{8,136,264,392},{16,144,272,400},{24,152,280,408},{32,1..., dimensions={0} | all-to-all | bytes 262144 | tf_op jit(solution)/shard_map/all_to_all | solution.py:307
  46.3 0.1 enter.1
  46.5 17.7 %all_to_all.26.s_ref = bf16[16,56,256]{2,1,0:T(8,128)(2,1)S(1)} all-to-all(bf16[16,56,256]{2,1,0:T(8,128)(2,1)S(1)} %enter.1), channel_id=1, replica_groups={{0,8,16,24,32,40,48,56,64,72,80,88,96,104,112,120},{128,136,144,152,160..., dimensions={0} | all-to-all | bytes 917504 | tf_op jit(solution)/shard_map/all_to_all | solution.py:307
  64.2 0.0 copy-start.3
  64.2 0.0 copy-start.4
  64.2 0.0 copy-start.5
  64.2 0.0 copy-start.8
  64.3 0.0 copy-start.9
  64.3 2.2 %collective-permute-start.1 = (bf16[16,32,256]{2,1,0:T(8,128)(2,1)S(1)}, bf16[16,32,256]{2,1,0:T(8,128)(2,1)S(1)}, u32[]{:S(2)}, u32[]{:S(2)}) collective-permute-start(bf16[16,32,256]{2,1,0:T(8,128)(2,1)S(1)} %slice.4.kv_ref), channel_id=1, source_target_pairs={{0,8},{8,0},{16,24},{24,16},{32,40},{40,32},{48,56},{56,48},{64,72... | collective-permute-start | bytes 786440 | tf_op jit(solution)/shard_map/ppermute | solution.py:347
  66.4 1.1 %attend_own.1 = (f32[128,1024]{1,0:T(8,128)S(1)}, f32[8,1024]{1,0:T(8,128)S(1)}) custom-call(bf16[128,1024]{1,0:T(8,128)(2,1)S(1)} %copy-done.1, bf16[272,256]{1,0:T(8,128)(2,1)S(1)} %collective-permute-done.got_ref.p_ref, bf16[16,32,256]{2,1,0:T(8,128)(2,1)S(1)} %slice.4.kv_ref), custom_call_target="tpu_custom_call" | custom-call | flops 300000000 | bytes 2000000 | tf_op jit(solution)/shard_map/attend_own/pallas_call | solution.py:294
  67.5 0.3 collective-permute-done.1.kv_ref
  67.8 1.8 %attend_other.1.after_ref = bf16[8,144,128]{2,1,0:T(8,128)(2,1)} custom-call(bf16[128,1024]{1,0:T(8,128)(2,1)S(1)} %copy-done.1, bf16[272,256]{1,0:T(8,128)(2,1)S(1)} %collective-permute-done.got_ref.p_ref, bf16[16,32,256]{2,1,0:T(8,128)(2,1)S(1)} %collective-permute-done.1.kv_ref, f32[128,1024]{1,0:T(8,128)S(1)} %get-tuple-element.13.sum_ref, ...), custom_call_target="tpu_custom_call" | custom-call | flops 300000000 | bytes 2000000 | tf_op jit(solution)/shard_map/attend_other/pallas_call | solution.py:294
  69.6 5.0 %all-to-all-start.3 = ((bf16[8,144,128]{2,1,0:T(8,128)(2,1)}), bf16[8,144,128]{2,1,0:T(8,128)(2,1)S(1)}, u32[]{:S(2)}, u32[]{:S(2)}) async-start(bf16[8,144,128]{2,1,0:T(8,128)(2,1)} %attend_other.1.after_ref), calls=%async_computation.3 | async-start | bytes 589824 | tf_op jit(solution)/shard_map/all_to_all | solution.py:307
  74.6 0.0 copy-done.4
  74.7 0.0 copy-start
  74.7 0.7 within.1
  75.4 0.7 copy-done
  76.1 0.6 carry.1.p_ref
  76.7 3.9 %all-to-all-done.3.rd_ref = bf16[8,144,128]{2,1,0:T(8,128)(2,1)S(1)} async-done(((bf16[8,144,128]{2,1,0:T(8,128)(2,1)}), bf16[8,144,128]{2,1,0:T(8,128)(2,1)S(1)}, u32[]{:S(2)}, u32[]{:S(2)}) %all-to-all-start.3) | async-done | bytes 294944 | tf_op jit(solution)/shard_map/all_to_all | solution.py:307
  80.6 0.4 project.1
  81.0 16.4 %all_to_all.27.re_ref = bf16[8,16,2048]{2,1,0:T(8,128)(2,1)S(1)} all-to-all(bf16[8,16,2048]{2,1,0:T(8,128)(2,1)S(1)} %project.1), channel_id=1, replica_groups=mesh['seq'=64,'tp'=8] {'tp'}, dimensions={0} | all-to-all | bytes 1048576 | tf_op jit(solution)/shard_map/all_to_all | solution.py:307
  97.4 0.7 total.1
  (10 shorter events, 0.0 us)
Async XLA Ops:
  2.4 17.1 %all-to-all-start = ((bf16[16,32,256]{2,1,0:T(8,128)(2,1)}), bf16[16,32,256]{2,1,0:T(8,128)(2,1)S(1)}, u32[]{:S(2)}, u32[]{:S(2)}) async-start(bf16[16,32,256]{2,1,0:T(8,128)(2,1)} %get-tuple-element.12), calls=%async_computation | async-start | bytes 524288 | tf_op jit(solution)/shard_map/all_to_all | solution.py:307
  9.5 57.0 %copy-start.1 = (bf16[128,1024]{1,0:T(8,128)(2,1)S(1)}, bf16[128,1024]{1,0:T(8,128)(2,1)}, u32[]{:S(2)}) copy-start(bf16[128,1024]{1,0:T(8,128)(2,1)} %q_ref.3) | copy-start | bytes 786436
  9.5 9.6 %collective-permute-start = (bf16[272,256]{1,0:T(8,128)(2,1)}, bf16[272,256]{1,0:T(8,128)(2,1)S(1)}, u32[]{:S(2)}, u32[]{:S(2)}) collective-permute-start(bf16[272,256]{1,0:T(8,128)(2,1)} %get-tuple-element.11), channel_id=1, source_target_pairs={{0,20},{1,21},{2,22},{3,23},{4,16},{5,17},{6,18},{7,19},{8,28},{9,... | collective-permute-start | bytes 417800 | tf_op jit(solution)/shard_map/ppermute | solution.py:331
  14.9 0.7 copy-start.6
  15.6 0.7 copy-start.7
  64.2 10.4 %copy-start.3 = (bf16[128,384]{1,0:T(8,128)(2,1)S(1)}, bf16[128,384]{1,0:T(8,128)(2,1)}, u32[]{:S(2)}) copy-start(bf16[128,384]{1,0:T(8,128)(2,1)} %x_ref.1) | copy-start | bytes 294916
  64.2 10.4 %copy-start.4 = (bf16[128,256]{1,0:T(8,128)(2,1)S(1)}, bf16[128,256]{1,0:T(8,128)(2,1)}, u32[]{:S(2)}) copy-start(bf16[128,256]{1,0:T(8,128)(2,1)} %b_ref.1) | copy-start | bytes 196612
  64.2 10.4 %copy-start.5 = (bf16[128,256]{1,0:T(8,128)(2,1)S(1)}, bf16[128,256]{1,0:T(8,128)(2,1)}, u32[]{:S(2)}) copy-start(bf16[128,256]{1,0:T(8,128)(2,1)} %c_ref.3) | copy-start | bytes 196612
  64.2 10.4 %copy-start.8 = (f32[128,6]{0,1:T(8,128)S(1)}, f32[128,6]{0,1:T(8,128)}, u32[]{:S(2)}) copy-start(f32[128,6]{0,1:T(8,128)} %param.17) | copy-start | bytes 9220
  64.3 10.4 %copy-start.9 = (bf16[128,384]{1,0:T(8,128)(2,1)S(1)}, bf16[128,384]{1,0:T(8,128)(2,1)}, u32[]{:S(2)}) copy-start(bf16[128,384]{1,0:T(8,128)(2,1)} %g_ref.1) | copy-start | bytes 294916
  64.3 3.6 %collective-permute-start.1 = (bf16[16,32,256]{2,1,0:T(8,128)(2,1)S(1)}, bf16[16,32,256]{2,1,0:T(8,128)(2,1)S(1)}, u32[]{:S(2)}, u32[]{:S(2)}) collective-permute-start(bf16[16,32,256]{2,1,0:T(8,128)(2,1)S(1)} %slice.4.kv_ref), channel_id=1, source_target_pairs={{0,8},{8,0},{16,24},{24,16},{32,40},{40,32},{48,56},{56,48},{64,72... | collective-permute-start | bytes 786440 | tf_op jit(solution)/shard_map/ppermute | solution.py:347
  69.6 11.0 %all-to-all-start.3 = ((bf16[8,144,128]{2,1,0:T(8,128)(2,1)}), bf16[8,144,128]{2,1,0:T(8,128)(2,1)S(1)}, u32[]{:S(2)}, u32[]{:S(2)}) async-start(bf16[8,144,128]{2,1,0:T(8,128)(2,1)} %attend_other.1.after_ref), calls=%async_computation.3 | async-start | bytes 589824 | tf_op jit(solution)/shard_map/all_to_all | solution.py:307
  74.7 1.4 %copy-start = (bf16[384,2048]{1,0:T(8,128)(2,1)S(1)}, bf16[384,2048]{1,0:T(8,128)(2,1)}, u32[]{:S(2)}) copy-start(bf16[384,2048]{1,0:T(8,128)(2,1)} %w_ref.2) | copy-start | bytes 4718596
  76.1 4.5 %copy-start.2 = (bf16[128,2048]{1,0:T(8,128)(2,1)S(1)}, bf16[128,2048]{1,0:T(8,128)(2,1)}, u32[]{:S(2)}) copy-start(bf16[128,2048]{1,0:T(8,128)(2,1)} %w_ref.3) | copy-start | bytes 1572868
